TPU v7x, 1024 devices: a whole 8x8x8 slice. The times are simulated.
1024 devices in a mesh: gx: 16 (over x_lo, y), gy: 64 (over x_hi, z, core).
Axes of the slice: x: 8 (x_hi: 4, x_lo: 2; x = x_hi * 2 + x_lo), y: 8, z: 8, core: 2. Of those that a mesh axis runs over, the one named last changes fastest.
Arguments:
- tokens: bfloat16 [1024, 18432], P('gy', 'gx'), may hold values from -6 to 6
- qkv_weight: bfloat16 [18432, 12800], P('gx', 'gy'), may hold values from -0.046875 to 0.046875
- out_weight: bfloat16 [12288, 18432], P(None, 'gy'), may hold values from -1.25 to 1.25
- cache: bfloat16 [1024, 2, 2048, 256], P(('gx', 'gy')), may hold values from -2000 to 2000
- cache_lengths: int32 [1024], P(('gx', 'gy')), may hold values from 16 to 2048, as said below
Outputs:
- mixed: bfloat16 [1024, 18432], P('gx', 'gy')
Inputs may be any that keep to these rules, and one draw needn't show every extreme that they name: `cache_lengths`: at least one sequence has exactly 2048 valid slots; lengths are spread from 16 to 2048 in scale.
All inputs are finite; a program needn't handle non-finite values.
Results may differ from a plain program's by a relative error of at most 0.01.
The roundings to bfloat16 on the way count: a program that leaves them out, or rounds other values in their place, can miss the bound.
Values may be sent and summed in bfloat16 or wider, within the bound.
No kernel may reach another device: no remote copies, remote signals or barrier semaphores. Data moves between devices by JAX's collectives and lax.ppermute only.
A program may use at most 32 MiB of HBM per device.

v0:
```python
import jax
import jax.numpy as jnp
from jax import lax
from jax.sharding import PartitionSpec as P

HEADS = 48
DH = 256


def rotate(vectors, token_position):
    half = vectors.shape[-1] // 2
    steps = jnp.arange(half).astype(jnp.float32)
    freqs = 10000.0 ** (-2.0 * steps / vectors.shape[-1])
    angle = token_position * freqs
    cosine = jnp.cos(angle)
    sine = jnp.sin(angle)
    first = vectors[..., :half]
    second = vectors[..., half:]
    return jnp.concatenate(
        [first * cosine - second * sine, second * cosine + first * sine], axis=-1
    )


def attend_cached_keys(proj, cache, cache_lengths):
    seq_here = proj.shape[0]
    width = HEADS * DH
    score_scale = DH ** (-0.5)
    token_position = cache_lengths.astype(jnp.float32)
    query_vector = proj[:, :width].astype(jnp.float32).reshape(seq_here, HEADS, DH)
    query_vector = rotate(query_vector, token_position[:, None, None]).astype(jnp.bfloat16)
    fresh_key = rotate(
        proj[:, width : width + DH].astype(jnp.float32), token_position[:, None]
    ).astype(jnp.bfloat16)
    fresh_value = proj[:, width + DH :]
    scores = (
        jnp.einsum("bpr,bar->bpa", query_vector, cache[:, 0], preferred_element_type=jnp.float32)
        * score_scale
    )
    valid = jnp.arange(cache.shape[2])[None, :] < cache_lengths[:, None]
    scores = jnp.where(valid[:, None, :], scores, -1e30)
    fresh = (
        jnp.einsum("shd,sd->sh", query_vector, fresh_key, preferred_element_type=jnp.float32)
        * score_scale
    )
    top = jnp.maximum(jnp.max(scores, axis=-1), fresh)
    expo = jnp.exp(scores - top[:, :, None])
    expo_fresh = jnp.exp(fresh - top)
    total = jnp.sum(expo, axis=-1) + expo_fresh
    softmax_weights = (expo / total[:, :, None]).astype(jnp.bfloat16)
    fresh_weight = (expo_fresh / total).astype(jnp.bfloat16)
    attended_output = jnp.einsum(
        "trj,tjp->trp", softmax_weights, cache[:, 1], preferred_element_type=jnp.float32
    )
    attended_output = (
        attended_output
        + fresh_weight.astype(jnp.float32)[:, :, None] * fresh_value.astype(jnp.float32)[:, None, :]
    )
    return attended_output.astype(jnp.bfloat16).reshape(seq_here, width)


def to_owner(summed):
    return lax.all_to_all(summed, "gy", split_axis=0, concat_axis=1, tiled=True)


def on_device(tokens, qkv_weight, out_weight, cache, cache_lengths):
    partial_value = jnp.dot(
        lax.all_gather(tokens, "gy", axis=0, tiled=True),
        qkv_weight,
        preferred_element_type=jnp.float32,
    )
    summed = lax.psum_scatter(partial_value, "gx", scatter_dimension=0, tiled=True).astype(
        jnp.bfloat16
    )
    proj = to_owner(summed)
    attended_output = attend_cached_keys(proj, cache, cache_lengths)
    mixed = jnp.dot(
        lax.all_gather(attended_output, "gy", axis=0, tiled=True),
        out_weight,
        preferred_element_type=jnp.float32,
    )
    return mixed.astype(jnp.bfloat16)


def solution(mesh):
    placed = (
        P("gy", "gx"),
        P("gx", "gy"),
        P(None, "gy"),
        P(("gx", "gy"), None, None, None),
        P(("gx", "gy")),
    )
    return jax.shard_map(
        on_device, mesh=mesh, in_specs=placed, out_specs=P("gx", "gy"), check_vma=False
    )
```

profile of v0, /device:TPU:1, one launch (start us, length us, event | category | flops | bytes accessed | tf_op | source)
XLA Modules:
  0.0 315.7 jit_solution(7609483700187465520)
XLA Ops:
  6.5 0.0 copy-start
  6.5 0.0 all-gather.4.cloned.1.call-start
  6.5 0.7 all-gather.4.cloned.1.call-update
  7.3 0.0 copy-start.1
  7.3 0.0 reduce-scatter.2.cloned.1.call-start
  7.3 108.7 %all-gather.4.cloned.1.call-done = bf16[1024,1152]{1,0:T(8,128)(2,1)} async-done(((bf16[16,1152]{1,0:T(8,128)(2,1)}), bf16[1024,1152]{1,0:T(8,128)(2,1)}) %all-gather.4.cloned.1.call-update) | async-done | bytes 2359312 | tf_op jit(solution)/shard_map/all_gather | solution.py:67
  116.0 0.0 copy-done
  116.0 3.5 %fusion.28 = f32[1024,200]{1,0:T(8,128)} fusion(bf16[1024,1152]{1,0:T(8,128)(2,1)} %all-gather.4.cloned.1.call-done, bf16[1152,200]{0,1:T(8,128)(2,1)S(1)} %copy-done), kind=kOutput, calls=%fused_computation.46 | convolution fusion | flops 471859200 | bytes 3639296 | tf_op jit(solution)/shard_map/dot_general | solution.py:66
  119.5 0.0 reduce-scatter.2.cloned.1.call-update
  120.2 60.7 %reduce-scatter.2.cloned.1.call-done = f32[64,200]{1,0:T(8,128)} async-done(((f32[1024,200]{1,0:T(8,128)}), f32[64,200]{1,0:T(8,128)}) %reduce-scatter.2.cloned.1.call-update) | async-done | bytes 51216 | tf_op jit(solution)/shard_map/reduce_scatter | solution.py:71
  180.9 0.8 convert_bitcast_fusion
  181.7 0.7 copy.8
  182.4 23.9 %all-to-all-start = ((bf16[64,1,200]{2,1,0:T(2,128)(2,1)}), bf16[64,1,200]{2,1,0:T(2,128)(2,1)S(1)}, u32[]{:S(2)}, u32[]{:S(2)}) async-start(bf16[64,1,200]{2,1,0:T(2,128)(2,1)} %copy.8), calls=%async_computation.1 | async-start | bytes 131072 | tf_op jit(solution)/shard_map/all_to_all | solution.py:62
  206.3 0.0 all-gather.6.cloned.1.call-start
  206.4 0.1 fusion.21
  206.4 12.2 %all-to-all-done = bf16[64,1,200]{2,1,0:T(2,128)(2,1)S(1)} async-done(((bf16[64,1,200]{2,1,0:T(2,128)(2,1)}), bf16[64,1,200]{2,1,0:T(2,128)(2,1)S(1)}, u32[]{:S(2)}, u32[]{:S(2)}) %all-to-all-start) | async-done | bytes 25632 | tf_op jit(solution)/shard_map/all_to_all | solution.py:62
  218.6 0.2 reduce.4
  218.8 0.1 all_to_all.14
  219.0 0.1 fusion.16
  219.1 0.1 convert_bitcast_fusion.2
  219.2 0.0 copy-done.1
  219.2 0.5 fusion.26
  219.8 0.1 fusion.27
  219.9 0.2 fusion.13
  220.2 0.4 fusion.7
  220.5 0.6 reshape.168
  221.2 0.0 all-gather.6.cloned.1.call-update
  221.2 80.7 %all-gather.6.cloned.1.call-done = bf16[64,1,12288]{2,1,0:T(2,128)(2,1)} async-done(((bf16[1,1,12288]{2,1,0:T(2,128)(2,1)}), bf16[64,1,12288]{2,1,0:T(2,128)(2,1)}) %all-gather.6.cloned.1.call-update) | async-done | bytes 1572880 | tf_op jit(solution)/shard_map/all_gather | solution.py:77
  301.9 7.3 %fusion.4 = bf16[64,288]{1,0:T(8,128)(2,1)} fusion(bf16[12288,288]{0,1:T(8,128)(2,1)} %param.7, bf16[64,1,12288]{2,1,0:T(2,128)(2,1)} %all-gather.6.cloned.1.call-done), kind=kOutput, calls=%fused_computation.5 | convolution fusion | flops 453003264 | bytes 8687616 | tf_op jit(solution)/shard_map/dot_general | solution.py:76
  (7 shorter events, 0.1 us)
Async XLA Ops:
  6.5 109.4 %copy-start = (bf16[1152,200]{0,1:T(8,128)(2,1)S(1)}, bf16[1152,200]{0,1:T(8,128)(2,1)}, u32[]{:S(2)}) copy-start(bf16[1152,200]{0,1:T(8,128)(2,1)} %param.6) | copy-start | bytes 1382404
  6.5 109.4 %all-gather.4.cloned.1.call-start = ((), (), s32[]{:S(2)}) async-start(), calls=%async_computation.2 | async-start | bytes 2396160 | tf_op jit(solution)/shard_map/all_gather | solution.py:67
  7.3 212.0 %copy-start.1 = (bf16[1,2,2048,256]{3,2,1,0:T(8,128)(2,1)S(1)}, bf16[1,2,2048,256]{3,2,1,0:T(8,128)(2,1)}, u32[]{:S(2)}) copy-start(bf16[1,2,2048,256]{3,2,1,0:T(8,128)(2,1)} %param.8) | copy-start | bytes 6291460
  7.3 173.6 %reduce-scatter.2.cloned.1.call-start = ((), (), s32[]{:S(2)}) async-start(), calls=%async_computation.3 | async-start | bytes 1114112 | tf_op jit(solution)/shard_map/reduce_scatter | solution.py:71
  182.4 36.3 %all-to-all-start = ((bf16[64,1,200]{2,1,0:T(2,128)(2,1)}), bf16[64,1,200]{2,1,0:T(2,128)(2,1)S(1)}, u32[]{:S(2)}, u32[]{:S(2)}) async-start(bf16[64,1,200]{2,1,0:T(2,128)(2,1)} %copy.8), calls=%async_computation.1 | async-start | bytes 131072 | tf_op jit(solution)/shard_map/all_to_all | solution.py:62
  206.3 95.5 %all-gather.6.cloned.1.call-start = ((), (), s32[]{:S(2)}) async-start(), calls=%async_computation.4 | async-start | bytes 3194880 | tf_op jit(solution)/shard_map/all_gather | solution.py:77
Sparse Core Ops, SparseCore 0:
  11.8 104.1 all-gather.3
  119.6 61.1 reduce-scatter.1
  221.3 80.5 all-gather.5
where the time goes:
time: 316 us
  waiting for transfers between devices  263 us (83%)
  starting transfers between devices  24 us (8%)
  between operations  13.9 us (4%)
  matrix products  11.8 us (4%)
    all_gather x1, waiting for transfers between devices, on_device(): lax.all_gather(tokens, 'gy', axis=0, tiled=True)  109 us
    all_gather x1, waiting for transfers between devices, on_device(): lax.all_gather(attended_output, 'gy', axis=0, tiled=True)  80.7 us
    reduce_scatter x1, waiting for transfers between devices, on_device(): lax.psum_scatter(partial_value, 'gx', scatter_dimension=0, tiled=True)  60.7 us
    all_to_all x1, starting transfers between devices, to_owner(): return lax.all_to_all(summed, 'gy', split_axis=0, concat_axis=1, tiled=True)  23.9 us
    all_to_all x1, waiting for transfers between devices, to_owner(): return lax.all_to_all(summed, 'gy', split_axis=0, concat_axis=1, tiled=True)  12.2 us
    dot_general x1, matrix products, on_device(): jnp.dot(lax.all_gather(attended_output, 'gy', axis=0, tiled=True), out_we...  7.31 us
  transfers between devices with their start and end apart: 4, of which 4 were waited for; matrix products, arithmetic and copies ran while one was open for 0% of the time, Pallas kernels for 0%

commit v1 on v0

--- a/solution.py
+++ b/solution.py
@@ -5,6 +5,10 @@
 
 HEADS = 48
 DH = 256
+
+CHIPS = 32
+PLANE = [[2 * chip + core for chip in range(CHIPS)] for core in range(2)]
+SIBLING = [(i, i ^ 1) for i in range(2 * CHIPS)]
 
 
 def rotate(vectors, token_position):
@@ -55,30 +59,47 @@
         attended_output
         + fresh_weight.astype(jnp.float32)[:, :, None] * fresh_value.astype(jnp.float32)[:, None, :]
     )
-    return attended_output.astype(jnp.bfloat16).reshape(seq_here, width)
+    return attended_output.astype(jnp.bfloat16)
 
 
-def to_owner(summed):
-    return lax.all_to_all(summed, "gy", split_axis=0, concat_axis=1, tiled=True)
+def over_plane(blocks):
+    return lax.all_to_all(
+        blocks, "gy", split_axis=0, concat_axis=0, axis_index_groups=PLANE, tiled=True
+    )
 
 
 def on_device(tokens, qkv_weight, out_weight, cache, cache_lengths):
-    partial_value = jnp.dot(
-        lax.all_gather(tokens, "gy", axis=0, tiled=True),
-        qkv_weight,
-        preferred_element_type=jnp.float32,
+    core = lax.rem(lax.axis_index("gy"), 2)
+    other_weight = lax.ppermute(qkv_weight, "gy", SIBLING)
+    pairs = tokens.reshape(8, 2, -1)
+    even, odd = pairs[:, 0], pairs[:, 1]
+    kept = jnp.where(core == 0, even, odd)
+    given = jnp.where(core == 0, odd, even)
+    taken = lax.ppermute(given, "gy", SIBLING)
+    rows = jnp.where(
+        core == 0,
+        jnp.concatenate([kept, taken], axis=0),
+        jnp.concatenate([taken, kept], axis=0),
     )
-    summed = lax.psum_scatter(partial_value, "gx", scatter_dimension=0, tiled=True).astype(
-        jnp.bfloat16
+    gathered = over_plane(jnp.broadcast_to(rows[None], (CHIPS,) + rows.shape))
+    gathered = gathered.reshape(CHIPS * 16, -1)
+    weights = jnp.concatenate([qkv_weight, other_weight], axis=1)
+    partial_value = jnp.dot(gathered, weights, preferred_element_type=jnp.float32)
+    parts = lax.all_to_all(
+        partial_value.reshape(16, 32, -1), "gx", split_axis=0, concat_axis=0, tiled=True
     )
-    proj = to_owner(summed)
-    attended_output = attend_cached_keys(proj, cache, cache_lengths)
-    mixed = jnp.dot(
-        lax.all_gather(attended_output, "gy", axis=0, tiled=True),
-        out_weight,
-        preferred_element_type=jnp.float32,
-    )
-    return mixed.astype(jnp.bfloat16)
+    summed = jnp.sum(parts, axis=0)
+    columns = summed.shape[1] // 2
+    summed = jnp.where(core == 0, summed, jnp.roll(summed, columns, axis=1)).astype(jnp.bfloat16)
+    proj = over_plane(summed).reshape(1, -1)
+    attended_output = attend_cached_keys(proj, cache, cache_lengths).reshape(1, 96, 128)
+    mine = over_plane(jnp.broadcast_to(attended_output, (CHIPS, 96, 128)))
+    theirs = lax.ppermute(mine, "gy", SIBLING)
+    both = jnp.concatenate([mine, theirs], axis=0).reshape(2 * CHIPS, -1)
+    mixed = jnp.dot(both, out_weight, preferred_element_type=jnp.float32).astype(jnp.bfloat16)
+    mixed = mixed.reshape(2, CHIPS, -1)
+    mixed = jnp.where(core == 0, mixed, mixed[::-1])
+    return mixed.transpose(1, 0, 2).reshape(2 * CHIPS, -1)
 
 
 def solution(mesh):

time: 316 us -> 160 us (0.51)
  the two profiles are of different devices: /device:TPU:1 before, /device:TPU:3 now
where the time goes in v1:
time: 160 us; the launch traced here: 159 us
  waiting for transfers between devices  66.8 us (42%)
  starting transfers between devices  47.7 us (30%)
  blocking collectives  29.3 us (18%)
  matrix products  8.29 us (5%)
  local copies, waits for them, and re-layouts  4.34 us (3%)
  other arithmetic  2.01 us (1%)
    all_to_all x2, waiting for transfers between devices, over_plane(): lax.all_to_all(blocks, 'gy', split_axis=0, concat_axis=0, axis_index_grou...  38.1 us
    all_to_all x1, blocking collectives, over_plane(): lax.all_to_all(blocks, 'gy', split_axis=0, concat_axis=0, axis_index_grou...  29.3 us
    all_to_all x2, starting transfers between devices, over_plane(): lax.all_to_all(blocks, 'gy', split_axis=0, concat_axis=0, axis_index_grou...  28.3 us
    all_to_all x1, waiting for transfers between devices, on_device(): lax.all_to_all(partial_value.reshape(16, 32, -1), 'gx', split_axis=0, con...  24.5 us
    all_to_all x1, starting transfers between devices, on_device(): lax.all_to_all(partial_value.reshape(16, 32, -1), 'gx', split_axis=0, con...  11.4 us
    dot_general x1, matrix products, on_device(): jnp.dot(both, out_weight, preferred_element_type=jnp.float32)  5.43 us
  transfers between devices with their start and end apart: 6, of which 6 were waited for; matrix products, arithmetic and copies ran while one was open for 0% of the time, Pallas kernels for 0%

profile of v1, /device:TPU:3, one launch (start us, length us, event | category | flops | bytes accessed | tf_op | source)
XLA Modules:
  0.0 159.5 jit_solution(5696252214756349895)
XLA Ops:
  0.0 0.8 reshape.246
  0.9 2.6 %collective-permute-start = (bf16[8,1152]{1,0:T(8,128)(2,1)S(1)}, bf16[8,1152]{1,0:T(8,128)(2,1)S(1)}, u32[]{:S(2)}, u32[]{:S(2)}) collective-permute-start(bf16[8,1152]{1,0:T(8,128)(2,1)S(1)} %bitcast.54), channel_id=1, source_target_pairs={{0,1},{1,0},{2,3},{3,2},{4,5},{5,4},{6,7},{7,6},{8,9},{9,8},{10,11... | collective-permute-start | bytes 55304 | tf_op jit(solution)/shard_map/ppermute | solution.py:78
  3.5 0.8 collective-permute-done
  4.3 1.1 broadcast_in_dim.19
  5.4 20.8 %all-to-all-start = ((bf16[32,16,1152]{2,1,0:T(8,128)(2,1)}), bf16[32,16,1152]{2,1,0:T(8,128)(2,1)S(1)}, u32[]{:S(2)}, u32[]{:S(2)}) async-start(bf16[32,16,1152]{2,1,0:T(8,128)(2,1)} %broadcast_in_dim.19), calls=%async_computation | async-start | bytes 2359296 | tf_op jit(solution)/shard_map/all_to_all | solution.py:66
  26.3 2.5 %collective-permute-start.1 = (bf16[1152,200]{0,1:T(8,128)(2,1)S(1)}, bf16[1152,200]{0,1:T(8,128)(2,1)S(1)}, u32[]{:S(2)}, u32[]{:S(2)}) collective-permute-start(bf16[1152,200]{0,1:T(8,128)(2,1)S(1)} %copy-done.1), channel_id=1, source_target_pairs={{0,1},{1,0},{2,3},{3,2},{4,5},{5,4},{6,7},{7,6},{8,9},{9,8},{10,11... | collective-permute-start | bytes 1382408 | tf_op jit(solution)/shard_map/ppermute | solution.py:73
  28.8 1.4 collective-permute-done.1
  30.2 27.1 %all-to-all-done = bf16[32,16,1152]{2,1,0:T(8,128)(2,1)S(1)} async-done(((bf16[32,16,1152]{2,1,0:T(8,128)(2,1)}), bf16[32,16,1152]{2,1,0:T(8,128)(2,1)S(1)}, u32[]{:S(2)}, u32[]{:S(2)}) %all-to-all-start) | async-done | bytes 1179680 | tf_op jit(solution)/shard_map/all_to_all | solution.py:66
  57.3 1.8 %fusion.13 = f32[16,32,400]{2,1,0:T(8,128)} fusion(bf16[16,32,1152]{2,1,0:T(8,128)(2,1)S(1)} %bitcast.50, bf16[1152,200]{0,1:T(8,128)(2,1)S(1)} %collective-permute-done.1, bf16[1152,200]{0,1:T(8,128)(2,1)S(1)} %copy-done.1), kind=kOutput, calls=%fused_computation.16 | convolution fusion | flops 473702400 | bytes 2920448 | tf_op jit(solution)/shard_map/dot_general | solution.py:87
  59.2 11.4 %all-to-all-start.1 = ((f32[16,32,400]{2,1,0:T(8,128)}), f32[16,32,400]{2,1,0:T(8,128)S(1)}, u32[]{:S(2)}, u32[]{:S(2)}) async-start(f32[16,32,400]{2,1,0:T(8,128)} %fusion.13), calls=%async_computation.1 | async-start | bytes 2097152 | tf_op jit(solution)/shard_map/all_to_all | solution.py:88
  71.4 24.5 %all-to-all-done.1 = f32[16,32,400]{2,1,0:T(8,128)S(1)} async-done(((f32[16,32,400]{2,1,0:T(8,128)}), f32[16,32,400]{2,1,0:T(8,128)S(1)}, u32[]{:S(2)}, u32[]{:S(2)}) %all-to-all-start.1) | async-done | bytes 819232 | tf_op jit(solution)/shard_map/all_to_all | solution.py:88
  96.1 0.2 fusion.19
  96.3 0.5 broadcast.141
  96.8 0.8 reduce.9
  97.7 0.7 reshape.272
  98.4 7.5 %all-to-all-start.2 = ((bf16[32,2,200]{2,1,0:T(2,128)(2,1)}), bf16[32,2,200]{2,1,0:T(2,128)(2,1)S(1)}, u32[]{:S(2)}, u32[]{:S(2)}) async-start(bf16[32,2,200]{2,1,0:T(2,128)(2,1)} %reshape.272), calls=%async_computation.2 | async-start | bytes 65536 | tf_op jit(solution)/shard_map/all_to_all | solution.py:66
  105.9 11.0 %all-to-all-done.2 = bf16[32,2,200]{2,1,0:T(2,128)(2,1)S(1)} async-done(((bf16[32,2,200]{2,1,0:T(2,128)(2,1)}), bf16[32,2,200]{2,1,0:T(2,128)(2,1)S(1)}, u32[]{:S(2)}, u32[]{:S(2)}) %all-to-all-start.2) | async-done | bytes 25632 | tf_op jit(solution)/shard_map/all_to_all | solution.py:66
  117.0 0.1 reshape.273
  117.1 0.2 reduce.4
  117.3 0.1 reshape.247
  117.4 0.1 fusion.21
  117.7 0.5 fusion.32
  118.2 0.1 fusion.33
  118.3 0.2 fusion.16
  118.6 0.4 fusion.7
  119.0 0.1 broadcast_in_dim.22
  119.1 29.3 %all_to_all.21 = bf16[32,96,128]{2,1,0:T(8,128)(2,1)S(1)} all-to-all(bf16[32,96,128]{2,1,0:T(8,128)(2,1)S(1)} %broadcast_in_dim.22), channel_id=1, replica_groups={{0,2,4,6,8,10,12,14,16,18,20,22,24,26,28,30,32,34,36,38,40,42,44,46,48,..., dimensions={0} | all-to-all | bytes 1572864 | tf_op jit(solution)/shard_map/all_to_all | solution.py:66
  148.4 2.8 %collective-permute-start.2 = (bf16[32,96,128]{2,1,0:T(8,128)(2,1)S(1)}, bf16[32,96,128]{2,1,0:T(8,128)(2,1)S(1)}, u32[]{:S(2)}, u32[]{:S(2)}) collective-permute-start(bf16[32,96,128]{2,1,0:T(8,128)(2,1)S(1)} %all_to_all.21), channel_id=1, source_target_pairs={{0,1},{1,0},{2,3},{3,2},{4,5},{5,4},{6,7},{7,6},{8,9},{9,8},{10,11... | collective-permute-start | bytes 2359304 | tf_op jit(solution)/shard_map/ppermute | solution.py:97
  151.3 1.9 %collective-permute-done.2 = bf16[32,96,128]{2,1,0:T(8,128)(2,1)S(1)} collective-permute-done((bf16[32,96,128]{2,1,0:T(8,128)(2,1)S(1)}, bf16[32,96,128]{2,1,0:T(8,128)(2,1)S(1)}, u32[]{:S(2)}, u32[]{:S(2)}) %collective-permute-start.2) | collective-permute-done | bytes 786464 | tf_op jit(solution)/shard_map/ppermute | solution.py:97
  153.1 0.1 pad_maximum_fusion
  153.3 5.4 %fusion.4 = bf16[64,288]{1,0:T(8,128)(2,1)S(1)} fusion(bf16[12288,288]{0,1:T(8,128)(2,1)} %param.7, bf16[8,8,96,128]{3,2,1,0:T(8,128)(2,1)S(1)} %bitcast.49), kind=kOutput, calls=%fused_computation.6 | convolution fusion | flops 453003264 | bytes 8687616 | tf_op jit(solution)/shard_map/dot_general | solution.py:99
  158.8 0.7 reshape.254
  (24 shorter events, 0.6 us)
Async XLA Ops:
  0.9 3.4 %collective-permute-start = (bf16[8,1152]{1,0:T(8,128)(2,1)S(1)}, bf16[8,1152]{1,0:T(8,128)(2,1)S(1)}, u32[]{:S(2)}, u32[]{:S(2)}) collective-permute-start(bf16[8,1152]{1,0:T(8,128)(2,1)S(1)} %bitcast.54), channel_id=1, source_target_pairs={{0,1},{1,0},{2,3},{3,2},{4,5},{5,4},{6,7},{7,6},{8,9},{9,8},{10,11... | collective-permute-start | bytes 55304 | tf_op jit(solution)/shard_map/ppermute | solution.py:78
  4.3 21.9 %copy-start.1 = (bf16[1152,200]{0,1:T(8,128)(2,1)S(1)}, bf16[1152,200]{0,1:T(8,128)(2,1)}, u32[]{:S(2)}) copy-start(bf16[1152,200]{0,1:T(8,128)(2,1)} %param.6) | copy-start | bytes 1382404
  5.4 51.9 %all-to-all-start = ((bf16[32,16,1152]{2,1,0:T(8,128)(2,1)}), bf16[32,16,1152]{2,1,0:T(8,128)(2,1)S(1)}, u32[]{:S(2)}, u32[]{:S(2)}) async-start(bf16[32,16,1152]{2,1,0:T(8,128)(2,1)} %broadcast_in_dim.19), calls=%async_computation | async-start | bytes 2359296 | tf_op jit(solution)/shard_map/all_to_all | solution.py:66
  26.3 4.0 %collective-permute-start.1 = (bf16[1152,200]{0,1:T(8,128)(2,1)S(1)}, bf16[1152,200]{0,1:T(8,128)(2,1)S(1)}, u32[]{:S(2)}, u32[]{:S(2)}) collective-permute-start(bf16[1152,200]{0,1:T(8,128)(2,1)S(1)} %copy-done.1), channel_id=1, source_target_pairs={{0,1},{1,0},{2,3},{3,2},{4,5},{5,4},{6,7},{7,6},{8,9},{9,8},{10,11... | collective-permute-start | bytes 1382408 | tf_op jit(solution)/shard_map/ppermute | solution.py:73
  59.2 36.8 %all-to-all-start.1 = ((f32[16,32,400]{2,1,0:T(8,128)}), f32[16,32,400]{2,1,0:T(8,128)S(1)}, u32[]{:S(2)}, u32[]{:S(2)}) async-start(f32[16,32,400]{2,1,0:T(8,128)} %fusion.13), calls=%async_computation.1 | async-start | bytes 2097152 | tf_op jit(solution)/shard_map/all_to_all | solution.py:88
  70.6 47.1 %copy-start = (bf16[1,2,2048,256]{3,2,1,0:T(8,128)(2,1)S(1)}, bf16[1,2,2048,256]{3,2,1,0:T(8,128)(2,1)}, u32[]{:S(2)}) copy-start(bf16[1,2,2048,256]{3,2,1,0:T(8,128)(2,1)} %param.8) | copy-start | bytes 6291460
  98.4 18.6 %all-to-all-start.2 = ((bf16[32,2,200]{2,1,0:T(2,128)(2,1)}), bf16[32,2,200]{2,1,0:T(2,128)(2,1)S(1)}, u32[]{:S(2)}, u32[]{:S(2)}) async-start(bf16[32,2,200]{2,1,0:T(2,128)(2,1)} %reshape.272), calls=%async_computation.2 | async-start | bytes 65536 | tf_op jit(solution)/shard_map/all_to_all | solution.py:66
  148.4 4.7 %collective-permute-start.2 = (bf16[32,96,128]{2,1,0:T(8,128)(2,1)S(1)}, bf16[32,96,128]{2,1,0:T(8,128)(2,1)S(1)}, u32[]{:S(2)}, u32[]{:S(2)}) collective-permute-start(bf16[32,96,128]{2,1,0:T(8,128)(2,1)S(1)} %all_to_all.21), channel_id=1, source_target_pairs={{0,1},{1,0},{2,3},{3,2},{4,5},{5,4},{6,7},{7,6},{8,9},{9,8},{10,11... | collective-permute-start | bytes 2359304 | tf_op jit(solution)/shard_map/ppermute | solution.py:97

commit v2 on v1

--- a/solution.py
+++ b/solution.py
@@ -9,6 +9,7 @@
 CHIPS = 32
 PLANE = [[2 * chip + core for chip in range(CHIPS)] for core in range(2)]
 SIBLING = [(i, i ^ 1) for i in range(2 * CHIPS)]
+NEXT_PLANE = [(i, i ^ 1) for i in range(16)]
 
 
 def rotate(vectors, token_position):
@@ -68,27 +69,35 @@
     )
 
 
+def swap_rows(rows, mine, axis, pairs):
+    split = rows.reshape((rows.shape[0] // 2, 2) + rows.shape[1:])
+    even, odd = split[:, 0], split[:, 1]
+    kept = jnp.where(mine == 0, even, odd)
+    return kept, lax.ppermute(jnp.where(mine == 0, odd, even), axis, pairs)
+
+
 def on_device(tokens, qkv_weight, out_weight, cache, cache_lengths):
     core = lax.rem(lax.axis_index("gy"), 2)
-    other_weight = lax.ppermute(qkv_weight, "gy", SIBLING)
-    pairs = tokens.reshape(8, 2, -1)
-    even, odd = pairs[:, 0], pairs[:, 1]
-    kept = jnp.where(core == 0, even, odd)
-    given = jnp.where(core == 0, odd, even)
-    taken = lax.ppermute(given, "gy", SIBLING)
+    plane = lax.rem(lax.axis_index("gx"), 2)
+    kept, taken = swap_rows(tokens, core, "gy", SIBLING)
     rows = jnp.where(
         core == 0,
         jnp.concatenate([kept, taken], axis=0),
         jnp.concatenate([taken, kept], axis=0),
     )
+    rows = jnp.concatenate(swap_rows(rows, plane, "gx", NEXT_PLANE), axis=1)
+    next_weight = lax.ppermute(qkv_weight, "gx", NEXT_PLANE)
+    own_columns = jnp.concatenate([qkv_weight, next_weight], axis=0)
+    weights = jnp.concatenate([own_columns, lax.ppermute(own_columns, "gy", SIBLING)], axis=1)
     gathered = over_plane(jnp.broadcast_to(rows[None], (CHIPS,) + rows.shape))
-    gathered = gathered.reshape(CHIPS * 16, -1)
-    weights = jnp.concatenate([qkv_weight, other_weight], axis=1)
-    partial_value = jnp.dot(gathered, weights, preferred_element_type=jnp.float32)
+    partial_value = jnp.dot(
+        gathered.reshape(CHIPS * 8, -1), weights, preferred_element_type=jnp.float32
+    )
     parts = lax.all_to_all(
-        partial_value.reshape(16, 32, -1), "gx", split_axis=0, concat_axis=0, tiled=True
+        partial_value.reshape(16, 16, -1), "gx", split_axis=0, concat_axis=0, tiled=True
     )
-    summed = jnp.sum(parts, axis=0)
+    summed = jnp.sum(parts.reshape((8, 2) + parts.shape[1:]), axis=0)
+    summed = summed.transpose(1, 0, 2).reshape(CHIPS, -1)
     columns = summed.shape[1] // 2
     summed = jnp.where(core == 0, summed, jnp.roll(summed, columns, axis=1)).astype(jnp.bfloat16)
     proj = over_plane(summed).reshape(1, -1)

time: 160 us -> 154 us (0.963)
  the two profiles are of different devices: /device:TPU:3 before, /device:TPU:19 now
where the time goes in v2:
time: 154 us; the launch traced here: 153 us
  starting transfers between devices  57.8 us (38%)
  waiting for transfers between devices  51.5 us (33%)
  blocking collectives  28.6 us (19%)
  matrix products  8.03 us (5%)
  local copies, waits for them, and re-layouts  4.56 us (3%)
  other arithmetic  1.76 us (1%)
    all_to_all x2, starting transfers between devices, over_plane(): lax.all_to_all(blocks, 'gy', split_axis=0, concat_axis=0, axis_index_grou...  29 us
    all_to_all x1, blocking collectives, over_plane(): lax.all_to_all(blocks, 'gy', split_axis=0, concat_axis=0, axis_index_grou...  28.6 us
    all_to_all x2, waiting for transfers between devices, over_plane(): lax.all_to_all(blocks, 'gy', split_axis=0, concat_axis=0, axis_index_grou...  19.1 us
    all_to_all x1, waiting for transfers between devices, on_device(): lax.all_to_all(partial_value.reshape(16, 16, -1), 'gx', split_axis=0, con...  14.9 us
    all_to_all x1, starting transfers between devices, on_device(): lax.all_to_all(partial_value.reshape(16, 16, -1), 'gx', split_axis=0, con...  14.6 us
    ppermute x1, waiting for transfers between devices, on_device(): next_weight = lax.ppermute(qkv_weight, 'gx', NEXT_PLANE)  10.2 us
    dot_general x1, matrix products, on_device(): jnp.dot(both, out_weight, preferred_element_type=jnp.float32)  5.43 us
    ppermute x2, starting transfers between devices, swap_rows(): return (kept, lax.ppermute(jnp.where(mine == 0, odd, even), axis, pairs))  4.68 us
  transfers between devices with their start and end apart: 8, of which 8 were waited for; matrix products, arithmetic and copies ran while one was open for 0% of the time, Pallas kernels for 0%

profile of v2, /device:TPU:19, one launch (start us, length us, event | category | flops | bytes accessed | tf_op | source)
XLA Modules:
  0.0 153.2 jit_solution(14736509470090538124)
XLA Ops:
  0.0 0.8 reshape.236
  0.9 2.6 %collective-permute-start = (bf16[8,1152]{1,0:T(8,128)(2,1)S(1)}, bf16[8,1152]{1,0:T(8,128)(2,1)S(1)}, u32[]{:S(2)}, u32[]{:S(2)}) collective-permute-start(bf16[8,1152]{1,0:T(8,128)(2,1)S(1)} %bitcast.62), channel_id=1, source_target_pairs={{0,1},{1,0},{2,3},{3,2},{4,5},{5,4},{6,7},{7,6},{8,9},{9,8},{10,11... | collective-permute-start | bytes 55304 | tf_op jit(solution)/shard_map/ppermute | solution.py:76
  3.5 0.8 collective-permute-done
  4.4 2.1 %collective-permute-start.1 = (bf16[8,1152]{1,0:T(8,128)(2,1)S(1)}, bf16[8,1152]{1,0:T(8,128)(2,1)S(1)}, u32[]{:S(2)}, u32[]{:S(2)}) collective-permute-start(bf16[8,1152]{1,0:T(8,128)(2,1)S(1)} %get-tuple-element.6), channel_id=1, source_target_pairs={{0,64},{64,0},{128,192},{192,128},{256,320},{320,256},{384,448},{4... | collective-permute-start | bytes 55304 | tf_op jit(solution)/shard_map/ppermute | solution.py:76
  6.6 2.5 %collective-permute-done.1 = bf16[8,1152]{1,0:T(8,128)(2,1)S(1)} collective-permute-done((bf16[8,1152]{1,0:T(8,128)(2,1)S(1)}, bf16[8,1152]{1,0:T(8,128)(2,1)S(1)}, u32[]{:S(2)}, u32[]{:S(2)}) %collective-permute-start.1) | collective-permute-done | bytes 18464 | tf_op jit(solution)/shard_map/ppermute | solution.py:76
  9.1 1.1 broadcast_in_dim.19
  10.2 20.8 %all-to-all-start = ((bf16[32,8,2304]{2,1,0:T(8,128)(2,1)}), bf16[32,8,2304]{2,1,0:T(8,128)(2,1)S(1)}, u32[]{:S(2)}, u32[]{:S(2)}) async-start(bf16[32,8,2304]{2,1,0:T(8,128)(2,1)} %broadcast_in_dim.19), calls=%async_computation | async-start | bytes 2359296 | tf_op jit(solution)/shard_map/all_to_all | solution.py:67
  31.0 2.0 %collective-permute-start.2 = (bf16[1152,200]{0,1:T(8,128)(2,1)S(1)}, bf16[1152,200]{0,1:T(8,128)(2,1)S(1)}, u32[]{:S(2)}, u32[]{:S(2)}) collective-permute-start(bf16[1152,200]{0,1:T(8,128)(2,1)S(1)} %copy-done), channel_id=1, source_target_pairs={{0,64},{64,0},{128,192},{192,128},{256,320},{320,256},{384,448},{4... | collective-permute-start | bytes 1382408 | tf_op jit(solution)/shard_map/ppermute | solution.py:89
  33.0 10.2 %collective-permute-done.2 = bf16[1152,200]{0,1:T(8,128)(2,1)S(1)} collective-permute-done((bf16[1152,200]{0,1:T(8,128)(2,1)S(1)}, bf16[1152,200]{0,1:T(8,128)(2,1)S(1)}, u32[]{:S(2)}, u32[]{:S(2)}) %collective-permute-start.2) | collective-permute-done | bytes 460832 | tf_op jit(solution)/shard_map/ppermute | solution.py:89
  43.2 4.6 %collective-permute-start.3 = (bf16[2304,200]{0,1:T(8,128)(2,1)S(1)}, bf16[2304,200]{0,1:T(8,128)(2,1)S(1)}, u32[]{:S(2)}, u32[]{:S(2)}) collective-permute-start(bf16[2304,200]{0,1:T(8,128)(2,1)S(1)} %constant_dynamic-update-slice_fusion), channel_id=1, source_target_pairs={{0,1},{1,0},{2,3},{3,2},{4,5},{5,4},{6,7},{7,6},{8,9},{9,8},{10,11... | collective-permute-start | bytes 2764808 | tf_op jit(solution)/shard_map/ppermute | solution.py:91
  47.9 2.1 %collective-permute-done.3 = bf16[2304,200]{0,1:T(8,128)(2,1)S(1)} collective-permute-done((bf16[2304,200]{0,1:T(8,128)(2,1)S(1)}, bf16[2304,200]{0,1:T(8,128)(2,1)S(1)}, u32[]{:S(2)}, u32[]{:S(2)}) %collective-permute-start.3) | collective-permute-done | bytes 921632 | tf_op jit(solution)/shard_map/ppermute | solution.py:91
  49.9 8.1 %all-to-all-done = bf16[32,8,2304]{2,1,0:T(8,128)(2,1)S(1)} async-done(((bf16[32,8,2304]{2,1,0:T(8,128)(2,1)}), bf16[32,8,2304]{2,1,0:T(8,128)(2,1)S(1)}, u32[]{:S(2)}, u32[]{:S(2)}) %all-to-all-start) | async-done | bytes 1179680 | tf_op jit(solution)/shard_map/all_to_all | solution.py:67
  58.0 1.6 %fusion.1 = f32[16,16,400]{2,1,0:T(8,128)} fusion(bf16[16,16,2304]{2,1,0:T(8,128)(2,1)S(1)} %bitcast.58, bf16[2304,200]{0,1:T(8,128)(2,1)S(1)} %collective-permute-done.3, bf16[2304,200]{0,1:T(8,128)(2,1)S(1)} %constant_dynamic-update-slice_fusion), kind=kOutput, calls=%fused_computation.3 | convolution fusion | flops 475545600 | bytes 3432448 | tf_op jit(solution)/shard_map/dot_general | solution.py:93
  59.6 14.6 %all-to-all-start.1 = ((f32[16,16,400]{2,1,0:T(8,128)}), f32[16,16,400]{2,1,0:T(8,128)S(1)}, u32[]{:S(2)}, u32[]{:S(2)}) async-start(f32[16,16,400]{2,1,0:T(8,128)} %fusion.1), calls=%async_computation.1 | async-start | bytes 1048576 | tf_op jit(solution)/shard_map/all_to_all | solution.py:96
  74.8 14.9 %all-to-all-done.1 = f32[16,16,400]{2,1,0:T(8,128)S(1)} async-done(((f32[16,16,400]{2,1,0:T(8,128)}), f32[16,16,400]{2,1,0:T(8,128)S(1)}, u32[]{:S(2)}, u32[]{:S(2)}) %all-to-all-start.1) | async-done | bytes 409632 | tf_op jit(solution)/shard_map/all_to_all | solution.py:96
  90.1 0.5 broadcast.142
  90.6 0.7 reduce.9
  91.3 0.7 reshape.265
  92.0 8.2 %all-to-all-start.2 = ((bf16[32,2,200]{2,1,0:T(2,128)(2,1)}), bf16[32,2,200]{2,1,0:T(2,128)(2,1)S(1)}, u32[]{:S(2)}, u32[]{:S(2)}) async-start(bf16[32,2,200]{2,1,0:T(2,128)(2,1)} %reshape.265), calls=%async_computation.2 | async-start | bytes 65536 | tf_op jit(solution)/shard_map/all_to_all | solution.py:67
  100.2 11.0 %all-to-all-done.2 = bf16[32,2,200]{2,1,0:T(2,128)(2,1)S(1)} async-done(((bf16[32,2,200]{2,1,0:T(2,128)(2,1)}), bf16[32,2,200]{2,1,0:T(2,128)(2,1)S(1)}, u32[]{:S(2)}, u32[]{:S(2)}) %all-to-all-start.2) | async-done | bytes 25632 | tf_op jit(solution)/shard_map/all_to_all | solution.py:67
  111.3 0.2 reduce.4
  111.5 0.1 reshape.240
  111.7 0.1 fusion.21
  111.9 0.5 fusion.33
  112.6 0.2 fusion.16
  112.9 0.4 fusion.10
  113.4 28.6 %all_to_all.21 = bf16[32,96,128]{2,1,0:T(8,128)(2,1)S(1)} all-to-all(bf16[32,96,128]{2,1,0:T(8,128)(2,1)S(1)} %broadcast_in_dim.22), channel_id=1, replica_groups={{0,2,4,6,8,10,12,14,16,18,20,22,24,26,28,30,32,34,36,38,40,42,44,46,48,..., dimensions={0} | all-to-all | bytes 1572864 | tf_op jit(solution)/shard_map/all_to_all | solution.py:67
  142.0 3.0 %collective-permute-start.4 = (bf16[32,96,128]{2,1,0:T(8,128)(2,1)S(1)}, bf16[32,96,128]{2,1,0:T(8,128)(2,1)S(1)}, u32[]{:S(2)}, u32[]{:S(2)}) collective-permute-start(bf16[32,96,128]{2,1,0:T(8,128)(2,1)S(1)} %all_to_all.21), channel_id=1, source_target_pairs={{0,1},{1,0},{2,3},{3,2},{4,5},{5,4},{6,7},{7,6},{8,9},{9,8},{10,11... | collective-permute-start | bytes 2359304 | tf_op jit(solution)/shard_map/ppermute | solution.py:106
  145.0 1.9 %collective-permute-done.4 = bf16[32,96,128]{2,1,0:T(8,128)(2,1)S(1)} collective-permute-done((bf16[32,96,128]{2,1,0:T(8,128)(2,1)S(1)}, bf16[32,96,128]{2,1,0:T(8,128)(2,1)S(1)}, u32[]{:S(2)}, u32[]{:S(2)}) %collective-permute-start.4) | collective-permute-done | bytes 786464 | tf_op jit(solution)/shard_map/ppermute | solution.py:106
  146.8 0.1 pad_maximum_fusion
  147.0 5.4 %fusion.7 = bf16[64,288]{1,0:T(8,128)(2,1)S(1)} fusion(bf16[12288,288]{0,1:T(8,128)(2,1)} %param.7, bf16[8,8,96,128]{3,2,1,0:T(8,128)(2,1)S(1)} %bitcast.56), kind=kOutput, calls=%fused_computation.10 | convolution fusion | flops 453003264 | bytes 8687616 | tf_op jit(solution)/shard_map/dot_general | solution.py:108
  152.5 0.7 reshape.247
  (35 shorter events, 1.2 us)
Async XLA Ops:
  0.9 3.4 %collective-permute-start = (bf16[8,1152]{1,0:T(8,128)(2,1)S(1)}, bf16[8,1152]{1,0:T(8,128)(2,1)S(1)}, u32[]{:S(2)}, u32[]{:S(2)}) collective-permute-start(bf16[8,1152]{1,0:T(8,128)(2,1)S(1)} %bitcast.62), channel_id=1, source_target_pairs={{0,1},{1,0},{2,3},{3,2},{4,5},{5,4},{6,7},{7,6},{8,9},{9,8},{10,11... | collective-permute-start | bytes 55304 | tf_op jit(solution)/shard_map/ppermute | solution.py:76
  4.4 26.6 %copy-start = (bf16[1152,200]{0,1:T(8,128)(2,1)S(1)}, bf16[1152,200]{0,1:T(8,128)(2,1)}, u32[]{:S(2)}) copy-start(bf16[1152,200]{0,1:T(8,128)(2,1)} %param.6) | copy-start | bytes 1382404
  4.4 4.6 %collective-permute-start.1 = (bf16[8,1152]{1,0:T(8,128)(2,1)S(1)}, bf16[8,1152]{1,0:T(8,128)(2,1)S(1)}, u32[]{:S(2)}, u32[]{:S(2)}) collective-permute-start(bf16[8,1152]{1,0:T(8,128)(2,1)S(1)} %get-tuple-element.6), channel_id=1, source_target_pairs={{0,64},{64,0},{128,192},{192,128},{256,320},{320,256},{384,448},{4... | collective-permute-start | bytes 55304 | tf_op jit(solution)/shard_map/ppermute | solution.py:76
  10.2 47.8 %all-to-all-start = ((bf16[32,8,2304]{2,1,0:T(8,128)(2,1)}), bf16[32,8,2304]{2,1,0:T(8,128)(2,1)S(1)}, u32[]{:S(2)}, u32[]{:S(2)}) async-start(bf16[32,8,2304]{2,1,0:T(8,128)(2,1)} %broadcast_in_dim.19), calls=%async_computation | async-start | bytes 2359296 | tf_op jit(solution)/shard_map/all_to_all | solution.py:67
  31.0 12.2 %collective-permute-start.2 = (bf16[1152,200]{0,1:T(8,128)(2,1)S(1)}, bf16[1152,200]{0,1:T(8,128)(2,1)S(1)}, u32[]{:S(2)}, u32[]{:S(2)}) collective-permute-start(bf16[1152,200]{0,1:T(8,128)(2,1)S(1)} %copy-done), channel_id=1, source_target_pairs={{0,64},{64,0},{128,192},{192,128},{256,320},{320,256},{384,448},{4... | collective-permute-start | bytes 1382408 | tf_op jit(solution)/shard_map/ppermute | solution.py:89
  43.2 6.7 %collective-permute-start.3 = (bf16[2304,200]{0,1:T(8,128)(2,1)S(1)}, bf16[2304,200]{0,1:T(8,128)(2,1)S(1)}, u32[]{:S(2)}, u32[]{:S(2)}) collective-permute-start(bf16[2304,200]{0,1:T(8,128)(2,1)S(1)} %constant_dynamic-update-slice_fusion), channel_id=1, source_target_pairs={{0,1},{1,0},{2,3},{3,2},{4,5},{5,4},{6,7},{7,6},{8,9},{9,8},{10,11... | collective-permute-start | bytes 2764808 | tf_op jit(solution)/shard_map/ppermute | solution.py:91
  59.6 52.4 %copy-start.1 = (bf16[1,2,2048,256]{3,2,1,0:T(8,128)(2,1)S(1)}, bf16[1,2,2048,256]{3,2,1,0:T(8,128)(2,1)}, u32[]{:S(2)}) copy-start(bf16[1,2,2048,256]{3,2,1,0:T(8,128)(2,1)} %param.8) | copy-start | bytes 6291460
  59.6 30.2 %all-to-all-start.1 = ((f32[16,16,400]{2,1,0:T(8,128)}), f32[16,16,400]{2,1,0:T(8,128)S(1)}, u32[]{:S(2)}, u32[]{:S(2)}) async-start(f32[16,16,400]{2,1,0:T(8,128)} %fusion.1), calls=%async_computation.1 | async-start | bytes 1048576 | tf_op jit(solution)/shard_map/all_to_all | solution.py:96
  92.0 19.2 %all-to-all-start.2 = ((bf16[32,2,200]{2,1,0:T(2,128)(2,1)}), bf16[32,2,200]{2,1,0:T(2,128)(2,1)S(1)}, u32[]{:S(2)}, u32[]{:S(2)}) async-start(bf16[32,2,200]{2,1,0:T(2,128)(2,1)} %reshape.265), calls=%async_computation.2 | async-start | bytes 65536 | tf_op jit(solution)/shard_map/all_to_all | solution.py:67
  142.0 4.9 %collective-permute-start.4 = (bf16[32,96,128]{2,1,0:T(8,128)(2,1)S(1)}, bf16[32,96,128]{2,1,0:T(8,128)(2,1)S(1)}, u32[]{:S(2)}, u32[]{:S(2)}) collective-permute-start(bf16[32,96,128]{2,1,0:T(8,128)(2,1)S(1)} %all_to_all.21), channel_id=1, source_target_pairs={{0,1},{1,0},{2,3},{3,2},{4,5},{5,4},{6,7},{7,6},{8,9},{9,8},{10,11... | collective-permute-start | bytes 2359304 | tf_op jit(solution)/shard_map/ppermute | solution.py:106

commit v3 on v2

--- a/solution.py
+++ b/solution.py
@@ -7,7 +7,40 @@
 DH = 256
 
 CHIPS = 32
-PLANE = [[2 * chip + core for chip in range(CHIPS)] for core in range(2)]
+
+
+def place(x_hi, z, core):
+    return (x_hi * 8 + z) * 2 + core
+
+
+def near_group(core, x_from, z_from):
+    members = {}
+    for dx in range(2):
+        for dz in range(2):
+            x_hi, z = (x_from + dx) % 4, (z_from + dz) % 8
+            members[x_hi % 2, z % 2] = place(x_hi, z, core)
+    return [members[key] for key in sorted(members)]
+
+
+PLANE = [[place(chip // 8, chip % 8, core) for chip in range(CHIPS)] for core in range(2)]
+NEAR = [
+    near_group(core, 2 * a + core, 2 * b + core)
+    for core in range(2)
+    for a in range(2)
+    for b in range(4)
+]
+FAR = [
+    [
+        (2 * pair + plane) * 64 + place(2 * a + e, 2 * b + w, core)
+        for plane in range(2)
+        for a in range(2)
+        for b in range(4)
+        for core in range(2)
+    ]
+    for pair in range(8)
+    for e in range(2)
+    for w in range(2)
+]
 SIBLING = [(i, i ^ 1) for i in range(2 * CHIPS)]
 NEXT_PLANE = [(i, i ^ 1) for i in range(16)]
 
@@ -63,46 +96,44 @@
     return attended_output.astype(jnp.bfloat16)
 
 
-def over_plane(blocks):
+def exchange(blocks, axis, groups):
     return lax.all_to_all(
-        blocks, "gy", split_axis=0, concat_axis=0, axis_index_groups=PLANE, tiled=True
+        blocks, axis, split_axis=0, concat_axis=0, axis_index_groups=groups, tiled=True
     )
-
-
-def swap_rows(rows, mine, axis, pairs):
-    split = rows.reshape((rows.shape[0] // 2, 2) + rows.shape[1:])
-    even, odd = split[:, 0], split[:, 1]
-    kept = jnp.where(mine == 0, even, odd)
-    return kept, lax.ppermute(jnp.where(mine == 0, odd, even), axis, pairs)
 
 
 def on_device(tokens, qkv_weight, out_weight, cache, cache_lengths):
     core = lax.rem(lax.axis_index("gy"), 2)
     plane = lax.rem(lax.axis_index("gx"), 2)
-    kept, taken = swap_rows(tokens, core, "gy", SIBLING)
-    rows = jnp.where(
-        core == 0,
-        jnp.concatenate([kept, taken], axis=0),
-        jnp.concatenate([taken, kept], axis=0),
+    width = tokens.shape[1]
+    split = tokens.reshape(4, 2, 2, width).transpose(1, 2, 0, 3)
+    far = jnp.broadcast_to(split[:, None], (2, 8, 2, 4, width)).reshape(CHIPS, 4, width)
+    far = exchange(far, ("gx", "gy"), FAR).reshape(2, 64, width)
+    rows = jnp.concatenate([far[0], far[1]], axis=1)
+    gathered = exchange(jnp.broadcast_to(rows[None], (4,) + rows.shape), "gy", NEAR)
+    next_weight = lax.ppermute(qkv_weight, "gx", NEXT_PLANE)
+    own_columns = jnp.concatenate(
+        [
+            jnp.where(plane == 0, qkv_weight, next_weight),
+            jnp.where(plane == 0, next_weight, qkv_weight),
+        ],
+        axis=0,
     )
-    rows = jnp.concatenate(swap_rows(rows, plane, "gx", NEXT_PLANE), axis=1)
-    next_weight = lax.ppermute(qkv_weight, "gx", NEXT_PLANE)
-    own_columns = jnp.concatenate([qkv_weight, next_weight], axis=0)
     weights = jnp.concatenate([own_columns, lax.ppermute(own_columns, "gy", SIBLING)], axis=1)
-    gathered = over_plane(jnp.broadcast_to(rows[None], (CHIPS,) + rows.shape))
     partial_value = jnp.dot(
-        gathered.reshape(CHIPS * 8, -1), weights, preferred_element_type=jnp.float32
+        gathered.reshape(256, 2 * width), weights, preferred_element_type=jnp.float32
     )
-    parts = lax.all_to_all(
-        partial_value.reshape(16, 16, -1), "gx", split_axis=0, concat_axis=0, tiled=True
-    )
-    summed = jnp.sum(parts.reshape((8, 2) + parts.shape[1:]), axis=0)
-    summed = summed.transpose(1, 0, 2).reshape(CHIPS, -1)
-    columns = summed.shape[1] // 2
-    summed = jnp.where(core == 0, summed, jnp.roll(summed, columns, axis=1)).astype(jnp.bfloat16)
-    proj = over_plane(summed).reshape(1, -1)
+    columns = partial_value.shape[1]
+    partial_value = partial_value.reshape(2, 2, 2, 4, 8, columns).transpose(2, 0, 3, 1, 4, 5)
+    parts = exchange(partial_value.reshape(16, 16, columns), "gx", None)
+    summed = jnp.sum(parts.reshape(8, 2, 16, columns), axis=0)
+    summed = summed.transpose(1, 0, 2).reshape(CHIPS, columns)
+    summed = jnp.where(core == 0, summed, jnp.roll(summed, columns // 2, axis=1))
+    summed = jnp.pad(summed.astype(jnp.bfloat16), ((0, 0), (0, 512 - columns)))
+    proj = exchange(summed.reshape(CHIPS, 4, 128), "gy", PLANE).reshape(CHIPS, 512)
+    proj = proj[:, :columns].reshape(1, -1)
     attended_output = attend_cached_keys(proj, cache, cache_lengths).reshape(1, 96, 128)
-    mine = over_plane(jnp.broadcast_to(attended_output, (CHIPS, 96, 128)))
+    mine = exchange(jnp.broadcast_to(attended_output, (CHIPS, 96, 128)), "gy", PLANE)
     theirs = lax.ppermute(mine, "gy", SIBLING)
     both = jnp.concatenate([mine, theirs], axis=0).reshape(2 * CHIPS, -1)
     mixed = jnp.dot(both, out_weight, preferred_element_type=jnp.float32).astype(jnp.bfloat16)

time: 154 us -> 147 us (0.955)
  starting transfers between devices: 57.8 us -> 46.8 us
  waiting for transfers between devices: 51.5 us -> 56.4 us
    all_to_all x3 -> x4, waiting for transfers between devices: 34 us -> 52.5 us  [exchange(): lax.all_to_all(blocks, axis, split_axis=0, concat_axis=0, axis_index_grou...]
    ppermute x1, waiting for transfers between devices: 10.2 us -> 0.01 us  [on_device(): next_weight = lax.ppermute(qkv_weight, 'gx', NEXT_PLANE)]
    ppermute x2 -> x0, starting transfers between devices: 4.68 us -> none  [swap_rows(): return (kept, lax.ppermute(jnp.where(mine == 0, odd, even), axis, pairs))]
    all_to_all x3 -> x4, starting transfers between devices: 43.6 us -> 39.6 us  [exchange(): lax.all_to_all(blocks, axis, split_axis=0, concat_axis=0, axis_index_grou...]
    ppermute x2 -> x0, waiting for transfers between devices: 3.33 us -> none  [swap_rows(): return (kept, lax.ppermute(jnp.where(mine == 0, odd, even), axis, pairs))]
    ppermute x1, starting transfers between devices: 4.61 us -> 2.35 us  [on_device(): lax.ppermute(own_columns, 'gy', SIBLING)]
  transfers between devices with their start and end apart: 8 -> 7, of which waited for: 8 -> 6; matrix products, arithmetic and copies ran while one was open for 0% -> 1% of each run, Pallas kernels for 0% -> 0%
where the time goes in v3:
time: 147 us
  waiting for transfers between devices  56.4 us (38%)
  starting transfers between devices  46.8 us (32%)
  blocking collectives  29 us (20%)
  matrix products  7.24 us (5%)
  local copies, waits for them, and re-layouts  5.48 us (4%)
    all_to_all x4, waiting for transfers between devices, exchange(): lax.all_to_all(blocks, axis, split_axis=0, concat_axis=0, axis_index_grou...  52.5 us
    all_to_all x4, starting transfers between devices, exchange(): lax.all_to_all(blocks, axis, split_axis=0, concat_axis=0, axis_index_grou...  39.6 us
    all_to_all x1, blocking collectives, exchange(): lax.all_to_all(blocks, axis, split_axis=0, concat_axis=0, axis_index_grou...  29 us
    dot_general x1, matrix products, on_device(): jnp.dot(both, out_weight, preferred_element_type=jnp.float32)  5.43 us
  transfers between devices with their start and end apart: 7, of which 6 were waited for; matrix products, arithmetic and copies ran while one was open for 1% of the time, Pallas kernels for 0%

profile of v3, /device:TPU:19, one launch (start us, length us, event | category | flops | bytes accessed | tf_op | source)
XLA Modules:
  0.0 146.9 jit_solution(3978594828767206137)
XLA Ops:
  0.0 0.8 reshape.197
  0.8 0.8 broadcast_in_dim.17
  1.6 21.7 %all-to-all-start = ((bf16[32,4,1152]{2,1,0:T(4,128)(2,1)}), bf16[32,4,1152]{2,1,0:T(4,128)(2,1)S(1)}, u32[]{:S(2)}, u32[]{:S(2)}) async-start(bf16[32,4,1152]{2,1,0:T(4,128)(2,1)} %bitcast.2), calls=%async_computation | async-start | bytes 589824 | tf_op jit(solution)/shard_map/all_to_all | solution.py:100
  23.3 2.0 %collective-permute-start = (bf16[1152,200]{0,1:T(8,128)(2,1)}, bf16[1152,200]{0,1:T(8,128)(2,1)S(1)}, u32[]{:S(2)}, u32[]{:S(2)}) collective-permute-start(bf16[1152,200]{0,1:T(8,128)(2,1)} %param.6), channel_id=1, source_target_pairs={{0,64},{64,0},{128,192},{192,128},{256,320},{320,256},{384,448},{4... | collective-permute-start | bytes 1382408 | tf_op jit(solution)/shard_map/ppermute | solution.py:114
  25.3 15.5 %all-to-all-done = bf16[32,4,1152]{2,1,0:T(4,128)(2,1)S(1)} async-done(((bf16[32,4,1152]{2,1,0:T(4,128)(2,1)}), bf16[32,4,1152]{2,1,0:T(4,128)(2,1)S(1)}, u32[]{:S(2)}, u32[]{:S(2)}) %all-to-all-start) | async-done | bytes 294944 | tf_op jit(solution)/shard_map/all_to_all | solution.py:100
  40.8 0.1 fusion.35
  41.1 1.1 broadcast_in_dim.18
  42.2 3.5 %all-to-all-start.1 = ((bf16[4,64,2304]{2,1,0:T(8,128)(2,1)}), bf16[4,64,2304]{2,1,0:T(8,128)(2,1)S(1)}, u32[]{:S(2)}, u32[]{:S(2)}) async-start(bf16[4,64,2304]{2,1,0:T(8,128)(2,1)} %broadcast_in_dim.18), calls=%async_computation.1 | async-start | bytes 2359296 | tf_op jit(solution)/shard_map/all_to_all | solution.py:100
  45.7 0.1 broadcast_select_fusion.1
  45.9 2.4 %collective-permute-start.1 = (bf16[2304,200]{0,1:T(8,128)(2,1)S(1)}, bf16[2304,200]{0,1:T(8,128)(2,1)S(1)}, u32[]{:S(2)}, u32[]{:S(2)}) collective-permute-start(bf16[2304,200]{0,1:T(8,128)(2,1)S(1)} %pad_maximum_fusion.1), channel_id=1, source_target_pairs={{0,1},{1,0},{2,3},{3,2},{4,5},{5,4},{6,7},{7,6},{8,9},{9,8},{10,11... | collective-permute-start | bytes 2764808 | tf_op jit(solution)/shard_map/ppermute | solution.py:122
  48.3 2.1 %collective-permute-done.1 = bf16[2304,200]{0,1:T(8,128)(2,1)S(1)} collective-permute-done((bf16[2304,200]{0,1:T(8,128)(2,1)S(1)}, bf16[2304,200]{0,1:T(8,128)(2,1)S(1)}, u32[]{:S(2)}, u32[]{:S(2)}) %collective-permute-start.1) | collective-permute-done | bytes 921632 | tf_op jit(solution)/shard_map/ppermute | solution.py:122
  50.4 10.9 %all-to-all-done.1 = bf16[4,64,2304]{2,1,0:T(8,128)(2,1)S(1)} async-done(((bf16[4,64,2304]{2,1,0:T(8,128)(2,1)}), bf16[4,64,2304]{2,1,0:T(8,128)(2,1)S(1)}, u32[]{:S(2)}, u32[]{:S(2)}) %all-to-all-start.1) | async-done | bytes 1179680 | tf_op jit(solution)/shard_map/all_to_all | solution.py:100
  61.3 0.8 fusion.9
  62.1 0.8 copy.15
  62.9 8.2 %all-to-all-start.2 = ((f32[16,16,400]{2,1,0:T(8,128)}), f32[16,16,400]{2,1,0:T(8,128)S(1)}, u32[]{:S(2)}, u32[]{:S(2)}) async-start(f32[16,16,400]{2,1,0:T(8,128)} %bitcast.7), calls=%async_computation.2 | async-start | bytes 1048576 | tf_op jit(solution)/shard_map/all_to_all | solution.py:100
  71.9 15.0 %all-to-all-done.2 = f32[16,16,400]{2,1,0:T(8,128)S(1)} async-done(((f32[16,16,400]{2,1,0:T(8,128)}), f32[16,16,400]{2,1,0:T(8,128)S(1)}, u32[]{:S(2)}, u32[]{:S(2)}) %all-to-all-start.2) | async-done | bytes 409632 | tf_op jit(solution)/shard_map/all_to_all | solution.py:100
  87.1 0.6 reshape.202
  87.8 6.1 %all-to-all-start.3 = ((bf16[32,4,128]{2,1,0:T(4,128)(2,1)}), bf16[32,4,128]{2,1,0:T(4,128)(2,1)S(1)}, u32[]{:S(2)}, u32[]{:S(2)}) async-start(bf16[32,4,128]{2,1,0:T(4,128)(2,1)} %reshape.202), calls=%async_computation.3 | async-start | bytes 65536 | tf_op jit(solution)/shard_map/all_to_all | solution.py:100
  93.9 11.0 %all-to-all-done.3 = bf16[32,4,128]{2,1,0:T(4,128)(2,1)S(1)} async-done(((bf16[32,4,128]{2,1,0:T(4,128)(2,1)}), bf16[32,4,128]{2,1,0:T(4,128)(2,1)S(1)}, u32[]{:S(2)}, u32[]{:S(2)}) %all-to-all-start.3) | async-done | bytes 32800 | tf_op jit(solution)/shard_map/all_to_all | solution.py:100
  105.0 0.1 reshape.204
  105.1 0.1 fusion.24
  105.4 0.5 fusion.37
  105.9 0.1 fusion.38
  106.0 0.2 fusion.19
  106.3 0.4 fusion.13
  106.7 0.1 broadcast_in_dim.25
  106.8 29.0 %all_to_all.25 = bf16[32,96,128]{2,1,0:T(8,128)(2,1)S(1)} all-to-all(bf16[32,96,128]{2,1,0:T(8,128)(2,1)S(1)} %broadcast_in_dim.25), channel_id=1, replica_groups={{0,2,4,6,8,10,12,14,16,18,20,22,24,26,28,30,32,34,36,38,40,42,44,46,48,..., dimensions={0} | all-to-all | bytes 1572864 | tf_op jit(solution)/shard_map/all_to_all | solution.py:100
  135.8 2.9 %collective-permute-start.2 = (bf16[32,96,128]{2,1,0:T(8,128)(2,1)S(1)}, bf16[32,96,128]{2,1,0:T(8,128)(2,1)S(1)}, u32[]{:S(2)}, u32[]{:S(2)}) collective-permute-start(bf16[32,96,128]{2,1,0:T(8,128)(2,1)S(1)} %all_to_all.25), channel_id=1, source_target_pairs={{0,1},{1,0},{2,3},{3,2},{4,5},{5,4},{6,7},{7,6},{8,9},{9,8},{10,11... | collective-permute-start | bytes 2359304 | tf_op jit(solution)/shard_map/ppermute | solution.py:137
  138.7 1.9 %collective-permute-done.2 = bf16[32,96,128]{2,1,0:T(8,128)(2,1)S(1)} collective-permute-done((bf16[32,96,128]{2,1,0:T(8,128)(2,1)S(1)}, bf16[32,96,128]{2,1,0:T(8,128)(2,1)S(1)}, u32[]{:S(2)}, u32[]{:S(2)}) %collective-permute-start.2) | collective-permute-done | bytes 786464 | tf_op jit(solution)/shard_map/ppermute | solution.py:137
  140.5 0.1 pad_maximum_fusion
  140.7 5.4 %fusion.10 = bf16[64,288]{1,0:T(8,128)(2,1)S(1)} fusion(bf16[12288,288]{0,1:T(8,128)(2,1)} %param.7, bf16[8,8,96,128]{3,2,1,0:T(8,128)(2,1)S(1)} %bitcast.56), kind=kOutput, calls=%fused_computation.13 | convolution fusion | flops 453003264 | bytes 8687616 | tf_op jit(solution)/shard_map/dot_general | solution.py:139
  146.2 0.7 reshape.211
  (29 shorter events, 0.7 us)
Async XLA Ops:
  1.6 39.2 %all-to-all-start = ((bf16[32,4,1152]{2,1,0:T(4,128)(2,1)}), bf16[32,4,1152]{2,1,0:T(4,128)(2,1)S(1)}, u32[]{:S(2)}, u32[]{:S(2)}) async-start(bf16[32,4,1152]{2,1,0:T(4,128)(2,1)} %bitcast.2), calls=%async_computation | async-start | bytes 589824 | tf_op jit(solution)/shard_map/all_to_all | solution.py:100
  23.3 22.4 %collective-permute-start = (bf16[1152,200]{0,1:T(8,128)(2,1)}, bf16[1152,200]{0,1:T(8,128)(2,1)S(1)}, u32[]{:S(2)}, u32[]{:S(2)}) collective-permute-start(bf16[1152,200]{0,1:T(8,128)(2,1)} %param.6), channel_id=1, source_target_pairs={{0,64},{64,0},{128,192},{192,128},{256,320},{320,256},{384,448},{4... | collective-permute-start | bytes 1382408 | tf_op jit(solution)/shard_map/ppermute | solution.py:114
  41.1 4.7 %copy-start = (bf16[1152,200]{0,1:T(8,128)(2,1)S(1)}, bf16[1152,200]{0,1:T(8,128)(2,1)}, u32[]{:S(2)}) copy-start(bf16[1152,200]{0,1:T(8,128)(2,1)} %param.6) | copy-start | bytes 1382404
  42.2 19.1 %all-to-all-start.1 = ((bf16[4,64,2304]{2,1,0:T(8,128)(2,1)}), bf16[4,64,2304]{2,1,0:T(8,128)(2,1)S(1)}, u32[]{:S(2)}, u32[]{:S(2)}) async-start(bf16[4,64,2304]{2,1,0:T(8,128)(2,1)} %broadcast_in_dim.18), calls=%async_computation.1 | async-start | bytes 2359296 | tf_op jit(solution)/shard_map/all_to_all | solution.py:100
  45.9 4.4 %collective-permute-start.1 = (bf16[2304,200]{0,1:T(8,128)(2,1)S(1)}, bf16[2304,200]{0,1:T(8,128)(2,1)S(1)}, u32[]{:S(2)}, u32[]{:S(2)}) collective-permute-start(bf16[2304,200]{0,1:T(8,128)(2,1)S(1)} %pad_maximum_fusion.1), channel_id=1, source_target_pairs={{0,1},{1,0},{2,3},{3,2},{4,5},{5,4},{6,7},{7,6},{8,9},{9,8},{10,11... | collective-permute-start | bytes 2764808 | tf_op jit(solution)/shard_map/ppermute | solution.py:122
  62.1 43.3 %copy-start.1 = (bf16[1,2,2048,256]{3,2,1,0:T(8,128)(2,1)S(1)}, bf16[1,2,2048,256]{3,2,1,0:T(8,128)(2,1)}, u32[]{:S(2)}) copy-start(bf16[1,2,2048,256]{3,2,1,0:T(8,128)(2,1)} %param.8) | copy-start | bytes 6291460
  62.9 23.9 %all-to-all-start.2 = ((f32[16,16,400]{2,1,0:T(8,128)}), f32[16,16,400]{2,1,0:T(8,128)S(1)}, u32[]{:S(2)}, u32[]{:S(2)}) async-start(f32[16,16,400]{2,1,0:T(8,128)} %bitcast.7), calls=%async_computation.2 | async-start | bytes 1048576 | tf_op jit(solution)/shard_map/all_to_all | solution.py:100
  87.8 17.2 %all-to-all-start.3 = ((bf16[32,4,128]{2,1,0:T(4,128)(2,1)}), bf16[32,4,128]{2,1,0:T(4,128)(2,1)S(1)}, u32[]{:S(2)}, u32[]{:S(2)}) async-start(bf16[32,4,128]{2,1,0:T(4,128)(2,1)} %reshape.202), calls=%async_computation.3 | async-start | bytes 65536 | tf_op jit(solution)/shard_map/all_to_all | solution.py:100
  135.8 4.8 %collective-permute-start.2 = (bf16[32,96,128]{2,1,0:T(8,128)(2,1)S(1)}, bf16[32,96,128]{2,1,0:T(8,128)(2,1)S(1)}, u32[]{:S(2)}, u32[]{:S(2)}) collective-permute-start(bf16[32,96,128]{2,1,0:T(8,128)(2,1)S(1)} %all_to_all.25), channel_id=1, source_target_pairs={{0,1},{1,0},{2,3},{3,2},{4,5},{5,4},{6,7},{7,6},{8,9},{9,8},{10,11... | collective-permute-start | bytes 2359304 | tf_op jit(solution)/shard_map/ppermute | solution.py:137

commit v4 on v3

--- a/solution.py
+++ b/solution.py
@@ -1,6 +1,8 @@
 import jax
 import jax.numpy as jnp
 from jax import lax
+from jax.experimental import pallas as pl
+from jax.experimental.pallas import tpu as pltpu
 from jax.sharding import PartitionSpec as P
 
 HEADS = 48
@@ -102,6 +104,58 @@
     )
 
 
+CHUNKS = 6
+
+
+def output_kernel(core_ref, mine_ref, theirs_ref, weights_ref, out_ref):
+    tiles = mine_ref.shape[1] // CHUNKS
+    depth = tiles * mine_ref.shape[2]
+    total = jnp.zeros((weights_ref.shape[0], 2 * CHIPS), jnp.float32)
+    for i in range(CHUNKS):
+        here = slice(i * tiles, (i + 1) * tiles)
+        rows = jnp.concatenate(
+            [
+                mine_ref[:, here, :].reshape(CHIPS, depth),
+                theirs_ref[:, here, :].reshape(CHIPS, depth),
+            ],
+            axis=0,
+        )
+        total += lax.dot_general(
+            weights_ref[:, i * depth : (i + 1) * depth],
+            rows,
+            (((1,), (1,)), ((), ())),
+            preferred_element_type=jnp.float32,
+        )
+    place_of = lax.broadcasted_iota(jnp.int32, (2 * CHIPS, 2 * CHIPS), 0)
+    row = lax.broadcasted_iota(jnp.int32, (2 * CHIPS, 2 * CHIPS), 1)
+    order = ((place_of >> 1) == (row & (CHIPS - 1))) & (
+        (place_of & 1) == ((row >> 5) ^ core_ref[0])
+    )
+    out_ref[...] = lax.dot_general(
+        order.astype(jnp.float32).astype(jnp.bfloat16),
+        total.astype(jnp.bfloat16),
+        (((1,), (1,)), ((), ())),
+        preferred_element_type=jnp.float32,
+    ).astype(jnp.bfloat16)
+
+
+def output_rows(core, mine, theirs, weights):
+    columns, depth = weights.shape
+    vmem = pl.BlockSpec(memory_space=pltpu.VMEM)
+    return pl.pallas_call(
+        output_kernel,
+        out_shape=jax.ShapeDtypeStruct((2 * CHIPS, columns), jnp.bfloat16),
+        in_specs=[pl.BlockSpec(memory_space=pltpu.SMEM), vmem, vmem, vmem],
+        out_specs=vmem,
+        compiler_params=pltpu.CompilerParams(vmem_limit_bytes=32 * 2**20),
+        cost_estimate=pl.CostEstimate(
+            flops=4 * CHIPS * columns * depth,
+            bytes_accessed=2 * columns * depth,
+            transcendentals=0,
+        ),
+    )(core.astype(jnp.int32).reshape(1), mine, theirs, weights)
+
+
 def on_device(tokens, qkv_weight, out_weight, cache, cache_lengths):
     core = lax.rem(lax.axis_index("gy"), 2)
     plane = lax.rem(lax.axis_index("gx"), 2)
@@ -135,11 +189,7 @@
     attended_output = attend_cached_keys(proj, cache, cache_lengths).reshape(1, 96, 128)
     mine = exchange(jnp.broadcast_to(attended_output, (CHIPS, 96, 128)), "gy", PLANE)
     theirs = lax.ppermute(mine, "gy", SIBLING)
-    both = jnp.concatenate([mine, theirs], axis=0).reshape(2 * CHIPS, -1)
-    mixed = jnp.dot(both, out_weight, preferred_element_type=jnp.float32).astype(jnp.bfloat16)
-    mixed = mixed.reshape(2, CHIPS, -1)
-    mixed = jnp.where(core == 0, mixed, mixed[::-1])
-    return mixed.transpose(1, 0, 2).reshape(2 * CHIPS, -1)
+    return output_rows(core, mine, theirs, out_weight.T)
 
 
 def solution(mesh):

time: 147 us -> 147 us (level)
  matrix products: 7.24 us -> 1.81 us
  Pallas kernels: 0 us -> 2.83 us
  local copies, waits for them, and re-layouts: 5.48 us -> 7.86 us
    dot_general x1 -> x0, matrix products: 5.43 us -> none  [on_device(): jnp.dot(both, out_weight, preferred_element_type=jnp.float32)]
    unnamed x5 -> x7, local copies, waits for them, and re-layouts: 0.02 us -> 3.05 us
    pallas_call x0 -> x1, Pallas kernels: none -> 2.83 us  [output_rows(): pl.pallas_call(output_kernel, out_shape=jax.ShapeDtypeStruct((2 * CHIPS,...]
where the time goes in v4:
time: 147 us; the launch traced here: 146 us
  waiting for transfers between devices  56.4 us (38%)
  starting transfers between devices  46.8 us (32%)
  blocking collectives  29 us (20%)
  local copies, waits for them, and re-layouts  7.86 us (5%)
  Pallas kernels  2.83 us (2%)
  matrix products  1.81 us (1%)
    all_to_all x4, waiting for transfers between devices, exchange(): lax.all_to_all(blocks, axis, split_axis=0, concat_axis=0, axis_index_grou...  52.5 us
    all_to_all x4, starting transfers between devices, exchange(): lax.all_to_all(blocks, axis, split_axis=0, concat_axis=0, axis_index_grou...  39.6 us
    all_to_all x1, blocking collectives, exchange(): lax.all_to_all(blocks, axis, split_axis=0, concat_axis=0, axis_index_grou...  29 us
    unnamed x7, local copies, waits for them, and re-layouts  3.05 us
  transfers between devices with their start and end apart: 7, of which 6 were waited for; matrix products, arithmetic and copies ran while one was open for 1% of the time, Pallas kernels for 0%

profile of v4, /device:TPU:19, one launch (start us, length us, event | category | flops | bytes accessed | tf_op | source)
XLA Modules:
  0.0 146.5 jit_solution(4282851148111733104)
XLA Ops:
  0.0 0.8 reshape.192
  0.8 0.8 broadcast_in_dim.17
  1.6 21.7 %all-to-all-start = ((bf16[32,4,1152]{2,1,0:T(4,128)(2,1)}), bf16[32,4,1152]{2,1,0:T(4,128)(2,1)S(1)}, u32[]{:S(2)}, u32[]{:S(2)}) async-start(bf16[32,4,1152]{2,1,0:T(4,128)(2,1)} %bitcast.3), calls=%async_computation | async-start | bytes 589824 | tf_op jit(solution)/shard_map/all_to_all | solution.py:102
  23.3 2.0 %collective-permute-start = (bf16[1152,200]{0,1:T(8,128)(2,1)}, bf16[1152,200]{0,1:T(8,128)(2,1)S(1)}, u32[]{:S(2)}, u32[]{:S(2)}) collective-permute-start(bf16[1152,200]{0,1:T(8,128)(2,1)} %param.6), channel_id=1, source_target_pairs={{0,64},{64,0},{128,192},{192,128},{256,320},{320,256},{384,448},{4... | collective-permute-start | bytes 1382408 | tf_op jit(solution)/shard_map/ppermute | solution.py:168
  25.3 15.5 %all-to-all-done = bf16[32,4,1152]{2,1,0:T(4,128)(2,1)S(1)} async-done(((bf16[32,4,1152]{2,1,0:T(4,128)(2,1)}), bf16[32,4,1152]{2,1,0:T(4,128)(2,1)S(1)}, u32[]{:S(2)}, u32[]{:S(2)}) %all-to-all-start) | async-done | bytes 294944 | tf_op jit(solution)/shard_map/all_to_all | solution.py:102
  40.8 0.1 fusion.28
  41.1 1.1 broadcast_in_dim.18
  42.2 3.5 %all-to-all-start.1 = ((bf16[4,64,2304]{2,1,0:T(8,128)(2,1)}), bf16[4,64,2304]{2,1,0:T(8,128)(2,1)S(1)}, u32[]{:S(2)}, u32[]{:S(2)}) async-start(bf16[4,64,2304]{2,1,0:T(8,128)(2,1)} %broadcast_in_dim.18), calls=%async_computation.1 | async-start | bytes 2359296 | tf_op jit(solution)/shard_map/all_to_all | solution.py:102
  45.7 0.1 broadcast_select_fusion.1
  46.0 2.4 %collective-permute-start.1 = (bf16[2304,200]{0,1:T(8,128)(2,1)S(1)}, bf16[2304,200]{0,1:T(8,128)(2,1)S(1)}, u32[]{:S(2)}, u32[]{:S(2)}) collective-permute-start(bf16[2304,200]{0,1:T(8,128)(2,1)S(1)} %pad_maximum_fusion), channel_id=1, source_target_pairs={{0,1},{1,0},{2,3},{3,2},{4,5},{5,4},{6,7},{7,6},{8,9},{9,8},{10,11... | collective-permute-start | bytes 2764808 | tf_op jit(solution)/shard_map/ppermute | solution.py:176
  48.3 2.1 %collective-permute-done.1 = bf16[2304,200]{0,1:T(8,128)(2,1)S(1)} collective-permute-done((bf16[2304,200]{0,1:T(8,128)(2,1)S(1)}, bf16[2304,200]{0,1:T(8,128)(2,1)S(1)}, u32[]{:S(2)}, u32[]{:S(2)}) %collective-permute-start.1) | collective-permute-done | bytes 921632 | tf_op jit(solution)/shard_map/ppermute | solution.py:176
  50.4 10.9 %all-to-all-done.1 = bf16[4,64,2304]{2,1,0:T(8,128)(2,1)S(1)} async-done(((bf16[4,64,2304]{2,1,0:T(8,128)(2,1)}), bf16[4,64,2304]{2,1,0:T(8,128)(2,1)S(1)}, u32[]{:S(2)}, u32[]{:S(2)}) %all-to-all-start.1) | async-done | bytes 1179680 | tf_op jit(solution)/shard_map/all_to_all | solution.py:102
  61.3 0.8 fusion.6
  62.1 0.8 copy.12
  63.0 8.2 %all-to-all-start.2 = ((f32[16,16,400]{2,1,0:T(8,128)}), f32[16,16,400]{2,1,0:T(8,128)S(1)}, u32[]{:S(2)}, u32[]{:S(2)}) async-start(f32[16,16,400]{2,1,0:T(8,128)} %bitcast.8), calls=%async_computation.2 | async-start | bytes 1048576 | tf_op jit(solution)/shard_map/all_to_all | solution.py:102
  71.9 15.0 %all-to-all-done.2 = f32[16,16,400]{2,1,0:T(8,128)S(1)} async-done(((f32[16,16,400]{2,1,0:T(8,128)}), f32[16,16,400]{2,1,0:T(8,128)S(1)}, u32[]{:S(2)}, u32[]{:S(2)}) %all-to-all-start.2) | async-done | bytes 409632 | tf_op jit(solution)/shard_map/all_to_all | solution.py:102
  87.1 0.1 fusion.16
  87.2 0.6 reshape.197
  87.8 6.1 %all-to-all-start.3 = ((bf16[32,4,128]{2,1,0:T(4,128)(2,1)}), bf16[32,4,128]{2,1,0:T(4,128)(2,1)S(1)}, u32[]{:S(2)}, u32[]{:S(2)}) async-start(bf16[32,4,128]{2,1,0:T(4,128)(2,1)} %reshape.197), calls=%async_computation.3 | async-start | bytes 65536 | tf_op jit(solution)/shard_map/all_to_all | solution.py:102
  94.0 11.0 %all-to-all-done.3 = bf16[32,4,128]{2,1,0:T(4,128)(2,1)S(1)} async-done(((bf16[32,4,128]{2,1,0:T(4,128)(2,1)}), bf16[32,4,128]{2,1,0:T(4,128)(2,1)S(1)}, u32[]{:S(2)}, u32[]{:S(2)}) %all-to-all-start.3) | async-done | bytes 32800 | tf_op jit(solution)/shard_map/all_to_all | solution.py:102
  105.0 0.1 reshape.199
  105.1 0.1 fusion.17
  105.4 0.5 fusion.30
  106.0 0.1 fusion.31
  106.1 0.2 fusion.13
  106.3 0.4 fusion.7
  106.7 0.1 broadcast_in_dim.25
  106.8 29.0 %all_to_all.25.mine_ref = bf16[32,96,128]{2,1,0:T(8,128)(2,1)S(1)} all-to-all(bf16[32,96,128]{2,1,0:T(8,128)(2,1)S(1)} %broadcast_in_dim.25), channel_id=1, replica_groups={{0,2,4,6,8,10,12,14,16,18,20,22,24,26,28,30,32,34,36,38,40,42,44,46,48,..., dimensions={0} | all-to-all | bytes 1572864 | tf_op jit(solution)/shard_map/all_to_all | solution.py:102
  135.8 2.9 %collective-permute-start.2 = (bf16[32,96,128]{2,1,0:T(8,128)(2,1)S(1)}, bf16[32,96,128]{2,1,0:T(8,128)(2,1)S(1)}, u32[]{:S(2)}, u32[]{:S(2)}) collective-permute-start(bf16[32,96,128]{2,1,0:T(8,128)(2,1)S(1)} %all_to_all.25.mine_ref), channel_id=1, source_target_pairs={{0,1},{1,0},{2,3},{3,2},{4,5},{5,4},{6,7},{7,6},{8,9},{9,8},{10,11... | collective-permute-start | bytes 2359304 | tf_op jit(solution)/shard_map/ppermute | solution.py:191
  138.7 1.9 %collective-permute-done.2.theirs_ref = bf16[32,96,128]{2,1,0:T(8,128)(2,1)S(1)} collective-permute-done((bf16[32,96,128]{2,1,0:T(8,128)(2,1)S(1)}, bf16[32,96,128]{2,1,0:T(8,128)(2,1)S(1)}, u32[]{:S(2)}, u32[]{:S(2)}) %collective-permute-start.2) | collective-permute-done | bytes 786464 | tf_op jit(solution)/shard_map/ppermute | solution.py:191
  140.6 3.0 %copy-done = bf16[12288,288]{0,1:T(8,128)(2,1)S(1)} copy-done((bf16[12288,288]{0,1:T(8,128)(2,1)S(1)}, bf16[12288,288]{0,1:T(8,128)(2,1)}, u32[]{:S(2)}) %copy-start) | copy-done | bytes 7077912
  143.6 2.8 %shard_map.55 = bf16[64,288]{1,0:T(8,128)(2,1)} custom-call(s32[1]{0:T(128)} %bitcast.core_ref, bf16[32,96,128]{2,1,0:T(8,128)(2,1)S(1)} %all_to_all.25.mine_ref, bf16[32,96,128]{2,1,0:T(8,128)(2,1)S(1)} %collective-permute-done.2.theirs_ref, bf16[288,12288]{1,0:T(8,128)(2,1)S(1)} %bitcast.48), custom_call_target="tpu_custom_call" | custom-call | flops 452984832 | bytes 7077888 | tf_op jit(solution)/shard_map/pallas_call | solution.py:145
  (27 shorter events, 0.6 us)
Async XLA Ops:
  1.6 39.2 %all-to-all-start = ((bf16[32,4,1152]{2,1,0:T(4,128)(2,1)}), bf16[32,4,1152]{2,1,0:T(4,128)(2,1)S(1)}, u32[]{:S(2)}, u32[]{:S(2)}) async-start(bf16[32,4,1152]{2,1,0:T(4,128)(2,1)} %bitcast.3), calls=%async_computation | async-start | bytes 589824 | tf_op jit(solution)/shard_map/all_to_all | solution.py:102
  23.3 22.4 %collective-permute-start = (bf16[1152,200]{0,1:T(8,128)(2,1)}, bf16[1152,200]{0,1:T(8,128)(2,1)S(1)}, u32[]{:S(2)}, u32[]{:S(2)}) collective-permute-start(bf16[1152,200]{0,1:T(8,128)(2,1)} %param.6), channel_id=1, source_target_pairs={{0,64},{64,0},{128,192},{192,128},{256,320},{320,256},{384,448},{4... | collective-permute-start | bytes 1382408 | tf_op jit(solution)/shard_map/ppermute | solution.py:168
  41.1 4.7 %copy-start.1 = (bf16[1152,200]{0,1:T(8,128)(2,1)S(1)}, bf16[1152,200]{0,1:T(8,128)(2,1)}, u32[]{:S(2)}) copy-start(bf16[1152,200]{0,1:T(8,128)(2,1)} %param.6) | copy-start | bytes 1382404
  42.2 19.1 %all-to-all-start.1 = ((bf16[4,64,2304]{2,1,0:T(8,128)(2,1)}), bf16[4,64,2304]{2,1,0:T(8,128)(2,1)S(1)}, u32[]{:S(2)}, u32[]{:S(2)}) async-start(bf16[4,64,2304]{2,1,0:T(8,128)(2,1)} %broadcast_in_dim.18), calls=%async_computation.1 | async-start | bytes 2359296 | tf_op jit(solution)/shard_map/all_to_all | solution.py:102
  46.0 4.4 %collective-permute-start.1 = (bf16[2304,200]{0,1:T(8,128)(2,1)S(1)}, bf16[2304,200]{0,1:T(8,128)(2,1)S(1)}, u32[]{:S(2)}, u32[]{:S(2)}) collective-permute-start(bf16[2304,200]{0,1:T(8,128)(2,1)S(1)} %pad_maximum_fusion), channel_id=1, source_target_pairs={{0,1},{1,0},{2,3},{3,2},{4,5},{5,4},{6,7},{7,6},{8,9},{9,8},{10,11... | collective-permute-start | bytes 2764808 | tf_op jit(solution)/shard_map/ppermute | solution.py:176
  62.1 43.3 %copy-start.2 = (bf16[1,2,2048,256]{3,2,1,0:T(8,128)(2,1)S(1)}, bf16[1,2,2048,256]{3,2,1,0:T(8,128)(2,1)}, u32[]{:S(2)}) copy-start(bf16[1,2,2048,256]{3,2,1,0:T(8,128)(2,1)} %param.8) | copy-start | bytes 6291460
  63.0 23.9 %all-to-all-start.2 = ((f32[16,16,400]{2,1,0:T(8,128)}), f32[16,16,400]{2,1,0:T(8,128)S(1)}, u32[]{:S(2)}, u32[]{:S(2)}) async-start(f32[16,16,400]{2,1,0:T(8,128)} %bitcast.8), calls=%async_computation.2 | async-start | bytes 1048576 | tf_op jit(solution)/shard_map/all_to_all | solution.py:102
  87.8 17.2 %all-to-all-start.3 = ((bf16[32,4,128]{2,1,0:T(4,128)(2,1)}), bf16[32,4,128]{2,1,0:T(4,128)(2,1)S(1)}, u32[]{:S(2)}, u32[]{:S(2)}) async-start(bf16[32,4,128]{2,1,0:T(4,128)(2,1)} %reshape.197), calls=%async_computation.3 | async-start | bytes 65536 | tf_op jit(solution)/shard_map/all_to_all | solution.py:102
  135.8 4.8 %collective-permute-start.2 = (bf16[32,96,128]{2,1,0:T(8,128)(2,1)S(1)}, bf16[32,96,128]{2,1,0:T(8,128)(2,1)S(1)}, u32[]{:S(2)}, u32[]{:S(2)}) collective-permute-start(bf16[32,96,128]{2,1,0:T(8,128)(2,1)S(1)} %all_to_all.25.mine_ref), channel_id=1, source_target_pairs={{0,1},{1,0},{2,3},{3,2},{4,5},{5,4},{6,7},{7,6},{8,9},{9,8},{10,11... | collective-permute-start | bytes 2359304 | tf_op jit(solution)/shard_map/ppermute | solution.py:191
  140.6 3.0 %copy-start = (bf16[12288,288]{0,1:T(8,128)(2,1)S(1)}, bf16[12288,288]{0,1:T(8,128)(2,1)}, u32[]{:S(2)}) copy-start(bf16[12288,288]{0,1:T(8,128)(2,1)} %param.7) | copy-start | bytes 21233668

commit v5 on v4

--- a/solution.py
+++ b/solution.py
@@ -20,7 +20,7 @@
     for dx in range(2):
         for dz in range(2):
             x_hi, z = (x_from + dx) % 4, (z_from + dz) % 8
-            members[x_hi % 2, z % 2] = place(x_hi, z, core)
+            members[z % 2, x_hi % 2] = place(x_hi, z, core)
     return [members[key] for key in sorted(members)]
 
 
@@ -43,6 +43,7 @@
     for e in range(2)
     for w in range(2)
 ]
+OWNERS = [[8 * a + 4 * e + b for e in range(2) for a in range(2) for b in range(4)]]
 SIBLING = [(i, i ^ 1) for i in range(2 * CHIPS)]
 NEXT_PLANE = [(i, i ^ 1) for i in range(16)]
 
@@ -139,6 +140,51 @@
     ).astype(jnp.bfloat16)
 
 
+def copy_kernel(core_ref, weights_ref, same_core_ref, copied_ref, sem):
+    copy = pltpu.make_async_copy(weights_ref, copied_ref, sem)
+    copy.start()
+    same_core_ref[0] = core_ref[0]
+    copy.wait()
+
+
+def copy_weights(core, weights):
+    smem = pl.BlockSpec(memory_space=pltpu.SMEM)
+    hbm = pl.BlockSpec(memory_space=pltpu.HBM)
+    return pl.pallas_call(
+        copy_kernel,
+        out_shape=(
+            jax.ShapeDtypeStruct(core.shape, core.dtype),
+            jax.ShapeDtypeStruct(weights.shape, weights.dtype),
+        ),
+        in_specs=[smem, hbm],
+        out_specs=(smem, hbm),
+        scratch_shapes=[pltpu.SemaphoreType.DMA],
+        compiler_params=pltpu.CompilerParams(vmem_limit_bytes=54 * 2**20),
+        cost_estimate=pl.CostEstimate(
+            flops=0, bytes_accessed=4 * weights.size, transcendentals=0
+        ),
+    )(core, weights)
+
+
+def hold_kernel(weights_ref, held_ref):
+    pass
+
+
+def hold(weights):
+    vmem = pl.BlockSpec(memory_space=pltpu.VMEM)
+    return pl.pallas_call(
+        hold_kernel,
+        out_shape=jax.ShapeDtypeStruct(weights.shape, weights.dtype),
+        in_specs=[vmem],
+        out_specs=vmem,
+        input_output_aliases={0: 0},
+        compiler_params=pltpu.CompilerParams(vmem_limit_bytes=46 * 2**20),
+        cost_estimate=pl.CostEstimate(
+            flops=0, bytes_accessed=2 * weights.size, transcendentals=0
+        ),
+    )(weights)
+
+
 def output_rows(core, mine, theirs, weights):
     columns, depth = weights.shape
     vmem = pl.BlockSpec(memory_space=pltpu.VMEM)
@@ -178,18 +224,25 @@
         gathered.reshape(256, 2 * width), weights, preferred_element_type=jnp.float32
     )
     columns = partial_value.shape[1]
-    partial_value = partial_value.reshape(2, 2, 2, 4, 8, columns).transpose(2, 0, 3, 1, 4, 5)
-    parts = exchange(partial_value.reshape(16, 16, columns), "gx", None)
-    summed = jnp.sum(parts.reshape(8, 2, 16, columns), axis=0)
-    summed = summed.transpose(1, 0, 2).reshape(CHIPS, columns)
-    summed = jnp.where(core == 0, summed, jnp.roll(summed, columns // 2, axis=1))
+    parts = lax.all_to_all(
+        partial_value.reshape(2, 16, 8, columns),
+        "gx",
+        split_axis=1,
+        concat_axis=1,
+        axis_index_groups=OWNERS,
+        tiled=True,
+    )
+    summed = jnp.sum(parts.reshape(2, 8, 2, 8, columns), axis=1)
+    summed = summed.transpose(0, 2, 1, 3).reshape(CHIPS, columns)
+    same_core, turned = copy_weights(core.astype(jnp.int32).reshape(1), out_weight.T)
+    summed = jnp.where(same_core[0] == 0, summed, jnp.roll(summed, columns // 2, axis=1))
     summed = jnp.pad(summed.astype(jnp.bfloat16), ((0, 0), (0, 512 - columns)))
     proj = exchange(summed.reshape(CHIPS, 4, 128), "gy", PLANE).reshape(CHIPS, 512)
     proj = proj[:, :columns].reshape(1, -1)
     attended_output = attend_cached_keys(proj, cache, cache_lengths).reshape(1, 96, 128)
     mine = exchange(jnp.broadcast_to(attended_output, (CHIPS, 96, 128)), "gy", PLANE)
     theirs = lax.ppermute(mine, "gy", SIBLING)
-    return output_rows(core, mine, theirs, out_weight.T)
+    return output_rows(core, mine, theirs, hold(turned))
 
 
 def solution(mesh):

time: 147 us -> 349 us (2.37)
  the two profiles are of different devices: /device:TPU:19 before, /device:TPU:3 now
where the time goes in v5:
time: 349 us
  Pallas kernels  219 us (63%)
  starting transfers between devices  49.4 us (14%)
  waiting for transfers between devices  38.9 us (11%)
  blocking collectives  29.7 us (9%)
  local copies, waits for them, and re-layouts  6.97 us (2%)
    pallas_call x1, Pallas kernels, copy_weights(): pl.pallas_call(copy_kernel, out_shape=(jax.ShapeDtypeStruct(core.shape, c...  216 us
    all_to_all x3, waiting for transfers between devices, exchange(): lax.all_to_all(blocks, axis, split_axis=0, concat_axis=0, axis_index_grou...  36.8 us
    all_to_all x3, starting transfers between devices, exchange(): lax.all_to_all(blocks, axis, split_axis=0, concat_axis=0, axis_index_grou...  33.3 us
    all_to_all x1, blocking collectives, exchange(): lax.all_to_all(blocks, axis, split_axis=0, concat_axis=0, axis_index_grou...  29.7 us
    all_to_all x1, starting transfers between devices, on_device(): lax.all_to_all(partial_value.reshape(2, 16, 8, columns), 'gx', split_axis...  7.57 us
  transfers between devices with their start and end apart: 7, of which 4 were waited for; matrix products, arithmetic and copies ran while one was open for 0% of the time, Pallas kernels for 62%

profile of v5, /device:TPU:3, one launch (start us, length us, event | category | flops | bytes accessed | tf_op | source)
XLA Modules:
  0.0 348.8 jit_solution(10361814456178591546)
XLA Ops:
  0.0 0.8 reshape.192
  0.8 0.8 broadcast_in_dim.17
  1.6 21.7 %all-to-all-start = ((bf16[32,4,1152]{2,1,0:T(4,128)(2,1)}), bf16[32,4,1152]{2,1,0:T(4,128)(2,1)S(1)}, u32[]{:S(2)}, u32[]{:S(2)}) async-start(bf16[32,4,1152]{2,1,0:T(4,128)(2,1)} %bitcast.5), calls=%async_computation | async-start | bytes 589824 | tf_op jit(solution)/shard_map/all_to_all | solution.py:103
  23.4 3.3 collective-permute-start
  26.7 15.0 %all-to-all-done = bf16[32,4,1152]{2,1,0:T(4,128)(2,1)S(1)} async-done(((bf16[32,4,1152]{2,1,0:T(4,128)(2,1)}), bf16[32,4,1152]{2,1,0:T(4,128)(2,1)S(1)}, u32[]{:S(2)}, u32[]{:S(2)}) %all-to-all-start) | async-done | bytes 294944 | tf_op jit(solution)/shard_map/all_to_all | solution.py:103
  41.7 0.1 fusion.28
  41.9 1.1 broadcast_in_dim.18
  43.0 3.5 %all-to-all-start.1 = ((bf16[4,64,2304]{2,1,0:T(8,128)(2,1)}), bf16[4,64,2304]{2,1,0:T(8,128)(2,1)S(1)}, u32[]{:S(2)}, u32[]{:S(2)}) async-start(bf16[4,64,2304]{2,1,0:T(8,128)(2,1)} %broadcast_in_dim.18), calls=%async_computation.1 | async-start | bytes 2359296 | tf_op jit(solution)/shard_map/all_to_all | solution.py:103
  46.6 0.1 broadcast_select_fusion.1
  46.7 0.1 pad_maximum_fusion
  46.8 2.6 collective-permute-start.1
  49.4 2.1 collective-permute-done.1
  51.5 10.7 %all-to-all-done.1 = bf16[4,64,2304]{2,1,0:T(8,128)(2,1)S(1)} async-done(((bf16[4,64,2304]{2,1,0:T(8,128)(2,1)}), bf16[4,64,2304]{2,1,0:T(8,128)(2,1)S(1)}, u32[]{:S(2)}, u32[]{:S(2)}) %all-to-all-start.1) | async-done | bytes 1179680 | tf_op jit(solution)/shard_map/all_to_all | solution.py:103
  62.2 1.6 fusion.1
  63.8 7.6 %all-to-all-start.2 = ((f32[2,16,8,400]{3,2,0,1:T(8,128)}), f32[2,16,8,400]{3,2,0,1:T(8,128)S(1)}, u32[]{:S(2)}, u32[]{:S(2)}) async-start(f32[2,16,8,400]{3,2,0,1:T(8,128)} %fusion.1), calls=%async_computation.2 | async-start | bytes 1048576 | tf_op jit(solution)/shard_map/all_to_all | solution.py:227
  72.0 216.0 %shard_map.55 = (s32[1]{0:T(128)}, bf16[288,12288]{1,0:T(8,128)(2,1)}) custom-call(s32[1]{0:T(128)} %bitcast.core_ref, bf16[288,12288]{1,0:T(8,128)(2,1)} %bitcast.42), custom_call_target="tpu_custom_call" | custom-call | bytes 14155776 | tf_op jit(solution)/shard_map/pallas_call | solution.py:153
  288.9 0.1 fusion.29
  289.0 0.1 fusion.16
  289.1 0.6 reshape.196
  289.7 8.1 %all-to-all-start.3 = ((bf16[32,4,128]{2,1,0:T(4,128)(2,1)}), bf16[32,4,128]{2,1,0:T(4,128)(2,1)S(1)}, u32[]{:S(2)}, u32[]{:S(2)}) async-start(bf16[32,4,128]{2,1,0:T(4,128)(2,1)} %reshape.196), calls=%async_computation.3 | async-start | bytes 65536 | tf_op jit(solution)/shard_map/all_to_all | solution.py:103
  297.8 11.0 %all-to-all-done.3 = bf16[32,4,128]{2,1,0:T(4,128)(2,1)S(1)} async-done(((bf16[32,4,128]{2,1,0:T(4,128)(2,1)}), bf16[32,4,128]{2,1,0:T(4,128)(2,1)S(1)}, u32[]{:S(2)}, u32[]{:S(2)}) %all-to-all-start.3) | async-done | bytes 32800 | tf_op jit(solution)/shard_map/all_to_all | solution.py:103
  308.9 0.1 reshape.198
  309.0 0.1 fusion.17
  309.3 0.5 fusion.30
  309.8 0.1 fusion.31
  309.9 0.2 fusion.13
  310.2 0.4 fusion.7
  310.6 0.1 broadcast_in_dim.25
  310.7 29.7 %all_to_all.25.mine_ref = bf16[32,96,128]{2,1,0:T(8,128)(2,1)S(1)} all-to-all(bf16[32,96,128]{2,1,0:T(8,128)(2,1)S(1)} %broadcast_in_dim.25), channel_id=1, replica_groups={{0,2,4,6,8,10,12,14,16,18,20,22,24,26,28,30,32,34,36,38,40,42,44,46,48,..., dimensions={0} | all-to-all | bytes 1572864 | tf_op jit(solution)/shard_map/all_to_all | solution.py:103
  340.4 2.6 collective-permute-start.2
  343.0 3.0 copy-done
  346.0 2.8 shard_map.57
  (28 shorter events, 0.5 us)
Async XLA Ops:
  1.6 40.1 %all-to-all-start = ((bf16[32,4,1152]{2,1,0:T(4,128)(2,1)}), bf16[32,4,1152]{2,1,0:T(4,128)(2,1)S(1)}, u32[]{:S(2)}, u32[]{:S(2)}) async-start(bf16[32,4,1152]{2,1,0:T(4,128)(2,1)} %bitcast.5), calls=%async_computation | async-start | bytes 589824 | tf_op jit(solution)/shard_map/all_to_all | solution.py:103
  23.4 23.2 %collective-permute-start = (bf16[1152,200]{0,1:T(8,128)(2,1)}, bf16[1152,200]{0,1:T(8,128)(2,1)S(1)}, u32[]{:S(2)}, u32[]{:S(2)}) collective-permute-start(bf16[1152,200]{0,1:T(8,128)(2,1)} %param.6), channel_id=1, source_target_pairs={{0,64},{64,0},{128,192},{192,128},{256,320},{320,256},{384,448},{4... | collective-permute-start | bytes 1382408 | tf_op jit(solution)/shard_map/ppermute | solution.py:214
  41.9 4.7 %copy-start.1 = (bf16[1152,200]{0,1:T(8,128)(2,1)S(1)}, bf16[1152,200]{0,1:T(8,128)(2,1)}, u32[]{:S(2)}) copy-start(bf16[1152,200]{0,1:T(8,128)(2,1)} %param.6) | copy-start | bytes 1382404
  43.0 19.2 %all-to-all-start.1 = ((bf16[4,64,2304]{2,1,0:T(8,128)(2,1)}), bf16[4,64,2304]{2,1,0:T(8,128)(2,1)S(1)}, u32[]{:S(2)}, u32[]{:S(2)}) async-start(bf16[4,64,2304]{2,1,0:T(8,128)(2,1)} %broadcast_in_dim.18), calls=%async_computation.1 | async-start | bytes 2359296 | tf_op jit(solution)/shard_map/all_to_all | solution.py:103
  46.8 4.7 %collective-permute-start.1 = (bf16[2304,200]{0,1:T(8,128)(2,1)S(1)}, bf16[2304,200]{0,1:T(8,128)(2,1)S(1)}, u32[]{:S(2)}, u32[]{:S(2)}) collective-permute-start(bf16[2304,200]{0,1:T(8,128)(2,1)S(1)} %pad_maximum_fusion), channel_id=1, source_target_pairs={{0,1},{1,0},{2,3},{3,2},{4,5},{5,4},{6,7},{7,6},{8,9},{9,8},{10,11... | collective-permute-start | bytes 2764808 | tf_op jit(solution)/shard_map/ppermute | solution.py:222
  63.8 224.9 %all-to-all-start.2 = ((f32[2,16,8,400]{3,2,0,1:T(8,128)}), f32[2,16,8,400]{3,2,0,1:T(8,128)S(1)}, u32[]{:S(2)}, u32[]{:S(2)}) async-start(f32[2,16,8,400]{3,2,0,1:T(8,128)} %fusion.1), calls=%async_computation.2 | async-start | bytes 1048576 | tf_op jit(solution)/shard_map/all_to_all | solution.py:227
  72.0 237.2 %copy-start.2 = (bf16[1,2,2048,256]{3,2,1,0:T(8,128)(2,1)S(1)}, bf16[1,2,2048,256]{3,2,1,0:T(8,128)(2,1)}, u32[]{:S(2)}) copy-start(bf16[1,2,2048,256]{3,2,1,0:T(8,128)(2,1)} %param.8) | copy-start | bytes 6291460
  289.7 19.2 %all-to-all-start.3 = ((bf16[32,4,128]{2,1,0:T(4,128)(2,1)}), bf16[32,4,128]{2,1,0:T(4,128)(2,1)S(1)}, u32[]{:S(2)}, u32[]{:S(2)}) async-start(bf16[32,4,128]{2,1,0:T(4,128)(2,1)} %reshape.196), calls=%async_computation.3 | async-start | bytes 65536 | tf_op jit(solution)/shard_map/all_to_all | solution.py:103
  340.4 5.6 %collective-permute-start.2 = (bf16[32,96,128]{2,1,0:T(8,128)(2,1)S(1)}, bf16[32,96,128]{2,1,0:T(8,128)(2,1)S(1)}, u32[]{:S(2)}, u32[]{:S(2)}) collective-permute-start(bf16[32,96,128]{2,1,0:T(8,128)(2,1)S(1)} %all_to_all.25.mine_ref), channel_id=1, source_target_pairs={{0,1},{1,0},{2,3},{3,2},{4,5},{5,4},{6,7},{7,6},{8,9},{9,8},{10,11... | collective-permute-start | bytes 2359304 | tf_op jit(solution)/shard_map/ppermute | solution.py:244
  343.0 3.0 copy-start

commit v6 on v5

--- a/solution.py
+++ b/solution.py
@@ -140,25 +140,23 @@
     ).astype(jnp.bfloat16)
 
 
-def copy_kernel(core_ref, weights_ref, same_core_ref, copied_ref, sem):
-    copy = pltpu.make_async_copy(weights_ref, copied_ref, sem)
-    copy.start()
+def copy_kernel(core_ref, weights_ref, same_core_ref, copied_ref):
     same_core_ref[0] = core_ref[0]
-    copy.wait()
+    copied_ref[...] = weights_ref[...]
 
 
 def copy_weights(core, weights):
     smem = pl.BlockSpec(memory_space=pltpu.SMEM)
-    hbm = pl.BlockSpec(memory_space=pltpu.HBM)
+    rows = pl.BlockSpec((32, weights.shape[1]), lambda step: (step, 0))
     return pl.pallas_call(
         copy_kernel,
         out_shape=(
             jax.ShapeDtypeStruct(core.shape, core.dtype),
             jax.ShapeDtypeStruct(weights.shape, weights.dtype),
         ),
-        in_specs=[smem, hbm],
-        out_specs=(smem, hbm),
-        scratch_shapes=[pltpu.SemaphoreType.DMA],
+        grid=(weights.shape[0] // 32,),
+        in_specs=[smem, rows],
+        out_specs=(smem, rows),
         compiler_params=pltpu.CompilerParams(vmem_limit_bytes=54 * 2**20),
         cost_estimate=pl.CostEstimate(
             flops=0, bytes_accessed=4 * weights.size, transcendentals=0

time: 349 us -> 145 us (0.42)
  the two profiles are of different devices: /device:TPU:3 before, /device:TPU:19 now
where the time goes in v6:
time: 145 us; the launch traced here: 144 us
  starting transfers between devices  47 us (32%)
  waiting for transfers between devices  43.9 us (30%)
  blocking collectives  29.2 us (20%)
  Pallas kernels  12.4 us (9%)
  local copies, waits for them, and re-layouts  6.97 us (5%)
  matrix products  2.61 us (2%)
  between operations  1.55 us (1%)
    all_to_all x3, waiting for transfers between devices, exchange(): lax.all_to_all(blocks, axis, split_axis=0, concat_axis=0, axis_index_grou...  37.5 us
    all_to_all x3, starting transfers between devices, exchange(): lax.all_to_all(blocks, axis, split_axis=0, concat_axis=0, axis_index_grou...  31.6 us
    all_to_all x1, blocking collectives, exchange(): lax.all_to_all(blocks, axis, split_axis=0, concat_axis=0, axis_index_grou...  29.2 us
    pallas_call x1, Pallas kernels, copy_weights(): pl.pallas_call(copy_kernel, out_shape=(jax.ShapeDtypeStruct(core.shape, c...  9.53 us
    all_to_all x1, starting transfers between devices, on_device(): lax.all_to_all(partial_value.reshape(2, 16, 8, columns), 'gx', split_axis...  8.24 us
    all_to_all x1, waiting for transfers between devices, on_device(): lax.all_to_all(partial_value.reshape(2, 16, 8, columns), 'gx', split_axis...  4.33 us
    unnamed x7, local copies, waits for them, and re-layouts  3.02 us
  transfers between devices with their start and end apart: 7, of which 5 were waited for; matrix products, arithmetic and copies ran while one was open for 1% of the time, Pallas kernels for 7%

profile of v6, /device:TPU:19, one launch (start us, length us, event | category | flops | bytes accessed | tf_op | source)
XLA Modules:
  0.0 144.4 jit_solution(5903781532492973110)
XLA Ops:
  0.0 0.8 reshape.192
  0.8 0.8 broadcast_in_dim.17
  1.6 21.7 %all-to-all-start = ((bf16[32,4,1152]{2,1,0:T(4,128)(2,1)}), bf16[32,4,1152]{2,1,0:T(4,128)(2,1)S(1)}, u32[]{:S(2)}, u32[]{:S(2)}) async-start(bf16[32,4,1152]{2,1,0:T(4,128)(2,1)} %bitcast.5), calls=%async_computation | async-start | bytes 589824 | tf_op jit(solution)/shard_map/all_to_all | solution.py:103
  23.3 2.0 %collective-permute-start = (bf16[1152,200]{0,1:T(8,128)(2,1)}, bf16[1152,200]{0,1:T(8,128)(2,1)S(1)}, u32[]{:S(2)}, u32[]{:S(2)}) collective-permute-start(bf16[1152,200]{0,1:T(8,128)(2,1)} %param.6), channel_id=1, source_target_pairs={{0,64},{64,0},{128,192},{192,128},{256,320},{320,256},{384,448},{4... | collective-permute-start | bytes 1382408 | tf_op jit(solution)/shard_map/ppermute | solution.py:212
  25.3 15.5 %all-to-all-done = bf16[32,4,1152]{2,1,0:T(4,128)(2,1)S(1)} async-done(((bf16[32,4,1152]{2,1,0:T(4,128)(2,1)}), bf16[32,4,1152]{2,1,0:T(4,128)(2,1)S(1)}, u32[]{:S(2)}, u32[]{:S(2)}) %all-to-all-start) | async-done | bytes 294944 | tf_op jit(solution)/shard_map/all_to_all | solution.py:103
  40.8 0.1 fusion.28
  41.1 1.1 broadcast_in_dim.18
  42.2 3.5 %all-to-all-start.1 = ((bf16[4,64,2304]{2,1,0:T(8,128)(2,1)}), bf16[4,64,2304]{2,1,0:T(8,128)(2,1)S(1)}, u32[]{:S(2)}, u32[]{:S(2)}) async-start(bf16[4,64,2304]{2,1,0:T(8,128)(2,1)} %broadcast_in_dim.18), calls=%async_computation.1 | async-start | bytes 2359296 | tf_op jit(solution)/shard_map/all_to_all | solution.py:103
  45.7 0.1 broadcast_select_fusion.1
  45.9 2.4 %collective-permute-start.1 = (bf16[2304,200]{0,1:T(8,128)(2,1)S(1)}, bf16[2304,200]{0,1:T(8,128)(2,1)S(1)}, u32[]{:S(2)}, u32[]{:S(2)}) collective-permute-start(bf16[2304,200]{0,1:T(8,128)(2,1)S(1)} %pad_maximum_fusion), channel_id=1, source_target_pairs={{0,1},{1,0},{2,3},{3,2},{4,5},{5,4},{6,7},{7,6},{8,9},{9,8},{10,11... | collective-permute-start | bytes 2764808 | tf_op jit(solution)/shard_map/ppermute | solution.py:220
  48.3 2.1 %collective-permute-done.1 = bf16[2304,200]{0,1:T(8,128)(2,1)S(1)} collective-permute-done((bf16[2304,200]{0,1:T(8,128)(2,1)S(1)}, bf16[2304,200]{0,1:T(8,128)(2,1)S(1)}, u32[]{:S(2)}, u32[]{:S(2)}) %collective-permute-start.1) | collective-permute-done | bytes 921632 | tf_op jit(solution)/shard_map/ppermute | solution.py:220
  50.4 10.9 %all-to-all-done.1 = bf16[4,64,2304]{2,1,0:T(8,128)(2,1)S(1)} async-done(((bf16[4,64,2304]{2,1,0:T(8,128)(2,1)}), bf16[4,64,2304]{2,1,0:T(8,128)(2,1)S(1)}, u32[]{:S(2)}, u32[]{:S(2)}) %all-to-all-start.1) | async-done | bytes 1179680 | tf_op jit(solution)/shard_map/all_to_all | solution.py:103
  61.3 1.6 %fusion.1 = f32[2,16,8,400]{3,2,0,1:T(8,128)} fusion(bf16[2304,200]{0,1:T(8,128)(2,1)S(1)} %collective-permute-done.1, bf16[1152,200]{0,1:T(8,128)(2,1)S(1)} %get-tuple-element.10, bf16[1152,200]{0,1:T(8,128)(2,1)S(1)} %get-tuple-element.9, bf16[2,16,8,2304]{3,2,1,0:T(8,128)(2,1)S(1)} %bitcast.44), kind=kOutput, calls=%fused_computation.3 | convolution fusion | flops 477388800 | bytes 3432448 | tf_op jit(solution)/shard_map/dot_general | solution.py:221
  62.9 8.2 %all-to-all-start.2 = ((f32[2,16,8,400]{3,2,0,1:T(8,128)}), f32[2,16,8,400]{3,2,0,1:T(8,128)S(1)}, u32[]{:S(2)}, u32[]{:S(2)}) async-start(f32[2,16,8,400]{3,2,0,1:T(8,128)} %fusion.1), calls=%async_computation.2 | async-start | bytes 1048576 | tf_op jit(solution)/shard_map/all_to_all | solution.py:225
  71.8 9.5 %shard_map.55 = (s32[1]{0:T(128)}, bf16[288,12288]{1,0:T(8,128)(2,1)}) custom-call(s32[1]{0:T(128)} %bitcast.core_ref, bf16[288,12288]{1,0:T(8,128)(2,1)} %bitcast.42), custom_call_target="tpu_custom_call" | custom-call | bytes 14155776 | tf_op jit(solution)/shard_map/pallas_call | solution.py:151
  82.0 4.3 %all-to-all-done.2 = f32[2,16,8,400]{3,2,0,1:T(8,128)S(1)} async-done(((f32[2,16,8,400]{3,2,0,1:T(8,128)}), f32[2,16,8,400]{3,2,0,1:T(8,128)S(1)}, u32[]{:S(2)}, u32[]{:S(2)}) %all-to-all-start.2) | async-done | bytes 409632 | tf_op jit(solution)/shard_map/all_to_all | solution.py:225
  86.5 0.1 fusion.29
  86.5 0.1 fusion.16
  86.6 0.6 reshape.196
  87.3 6.3 %all-to-all-start.3 = ((bf16[32,4,128]{2,1,0:T(4,128)(2,1)}), bf16[32,4,128]{2,1,0:T(4,128)(2,1)S(1)}, u32[]{:S(2)}, u32[]{:S(2)}) async-start(bf16[32,4,128]{2,1,0:T(4,128)(2,1)} %reshape.196), calls=%async_computation.3 | async-start | bytes 65536 | tf_op jit(solution)/shard_map/all_to_all | solution.py:103
  93.7 11.0 %all-to-all-done.3 = bf16[32,4,128]{2,1,0:T(4,128)(2,1)S(1)} async-done(((bf16[32,4,128]{2,1,0:T(4,128)(2,1)}), bf16[32,4,128]{2,1,0:T(4,128)(2,1)S(1)}, u32[]{:S(2)}, u32[]{:S(2)}) %all-to-all-start.3) | async-done | bytes 32800 | tf_op jit(solution)/shard_map/all_to_all | solution.py:103
  104.7 0.1 reshape.198
  104.9 0.1 fusion.17
  105.1 0.5 fusion.30
  105.7 0.1 fusion.31
  105.8 0.2 fusion.13
  106.0 0.4 fusion.7
  106.4 0.1 broadcast_in_dim.25
  106.5 29.2 %all_to_all.25.mine_ref = bf16[32,96,128]{2,1,0:T(8,128)(2,1)S(1)} all-to-all(bf16[32,96,128]{2,1,0:T(8,128)(2,1)S(1)} %broadcast_in_dim.25), channel_id=1, replica_groups={{0,2,4,6,8,10,12,14,16,18,20,22,24,26,28,30,32,34,36,38,40,42,44,46,48,..., dimensions={0} | all-to-all | bytes 1572864 | tf_op jit(solution)/shard_map/all_to_all | solution.py:103
  135.8 2.8 %collective-permute-start.2 = (bf16[32,96,128]{2,1,0:T(8,128)(2,1)S(1)}, bf16[32,96,128]{2,1,0:T(8,128)(2,1)S(1)}, u32[]{:S(2)}, u32[]{:S(2)}) collective-permute-start(bf16[32,96,128]{2,1,0:T(8,128)(2,1)S(1)} %all_to_all.25.mine_ref), channel_id=1, source_target_pairs={{0,1},{1,0},{2,3},{3,2},{4,5},{5,4},{6,7},{7,6},{8,9},{9,8},{10,11... | collective-permute-start | bytes 2359304 | tf_op jit(solution)/shard_map/ppermute | solution.py:242
  138.6 3.0 %copy-done = bf16[288,12288]{1,0:T(8,128)(2,1)S(1)} copy-done((bf16[288,12288]{1,0:T(8,128)(2,1)S(1)}, bf16[288,12288]{1,0:T(8,128)(2,1)}, u32[]{:S(2)}) %copy-start) | copy-done | bytes 7077912
  141.6 2.8 %shard_map.57 = bf16[64,288]{1,0:T(8,128)(2,1)} custom-call(s32[1]{0:T(128)} %bitcast.core_ref, bf16[32,96,128]{2,1,0:T(8,128)(2,1)S(1)} %all_to_all.25.mine_ref, bf16[32,96,128]{2,1,0:T(8,128)(2,1)S(1)} %collective-permute-done.2.theirs_ref, bf16[288,12288]{1,0:T(8,128)(2,1)S(1)} %shard_map.56.weights_ref), custom_call_target="tpu_custom_call" | custom-call | flops 452984832 | bytes 7077888 | tf_op jit(solution)/shard_map/pallas_call | solution.py:189
  (28 shorter events, 0.5 us)
Async XLA Ops:
  1.6 39.2 %all-to-all-start = ((bf16[32,4,1152]{2,1,0:T(4,128)(2,1)}), bf16[32,4,1152]{2,1,0:T(4,128)(2,1)S(1)}, u32[]{:S(2)}, u32[]{:S(2)}) async-start(bf16[32,4,1152]{2,1,0:T(4,128)(2,1)} %bitcast.5), calls=%async_computation | async-start | bytes 589824 | tf_op jit(solution)/shard_map/all_to_all | solution.py:103
  23.3 22.4 %collective-permute-start = (bf16[1152,200]{0,1:T(8,128)(2,1)}, bf16[1152,200]{0,1:T(8,128)(2,1)S(1)}, u32[]{:S(2)}, u32[]{:S(2)}) collective-permute-start(bf16[1152,200]{0,1:T(8,128)(2,1)} %param.6), channel_id=1, source_target_pairs={{0,64},{64,0},{128,192},{192,128},{256,320},{320,256},{384,448},{4... | collective-permute-start | bytes 1382408 | tf_op jit(solution)/shard_map/ppermute | solution.py:212
  41.1 4.7 %copy-start.1 = (bf16[1152,200]{0,1:T(8,128)(2,1)S(1)}, bf16[1152,200]{0,1:T(8,128)(2,1)}, u32[]{:S(2)}) copy-start(bf16[1152,200]{0,1:T(8,128)(2,1)} %param.6) | copy-start | bytes 1382404
  42.2 19.1 %all-to-all-start.1 = ((bf16[4,64,2304]{2,1,0:T(8,128)(2,1)}), bf16[4,64,2304]{2,1,0:T(8,128)(2,1)S(1)}, u32[]{:S(2)}, u32[]{:S(2)}) async-start(bf16[4,64,2304]{2,1,0:T(8,128)(2,1)} %broadcast_in_dim.18), calls=%async_computation.1 | async-start | bytes 2359296 | tf_op jit(solution)/shard_map/all_to_all | solution.py:103
  45.9 4.4 %collective-permute-start.1 = (bf16[2304,200]{0,1:T(8,128)(2,1)S(1)}, bf16[2304,200]{0,1:T(8,128)(2,1)S(1)}, u32[]{:S(2)}, u32[]{:S(2)}) collective-permute-start(bf16[2304,200]{0,1:T(8,128)(2,1)S(1)} %pad_maximum_fusion), channel_id=1, source_target_pairs={{0,1},{1,0},{2,3},{3,2},{4,5},{5,4},{6,7},{7,6},{8,9},{9,8},{10,11... | collective-permute-start | bytes 2764808 | tf_op jit(solution)/shard_map/ppermute | solution.py:220
  62.9 23.4 %all-to-all-start.2 = ((f32[2,16,8,400]{3,2,0,1:T(8,128)}), f32[2,16,8,400]{3,2,0,1:T(8,128)S(1)}, u32[]{:S(2)}, u32[]{:S(2)}) async-start(f32[2,16,8,400]{3,2,0,1:T(8,128)} %fusion.1), calls=%async_computation.2 | async-start | bytes 1048576 | tf_op jit(solution)/shard_map/all_to_all | solution.py:225
  71.8 33.3 %copy-start.2 = (bf16[1,2,2048,256]{3,2,1,0:T(8,128)(2,1)S(1)}, bf16[1,2,2048,256]{3,2,1,0:T(8,128)(2,1)}, u32[]{:S(2)}) copy-start(bf16[1,2,2048,256]{3,2,1,0:T(8,128)(2,1)} %param.8) | copy-start | bytes 6291460
  87.3 17.4 %all-to-all-start.3 = ((bf16[32,4,128]{2,1,0:T(4,128)(2,1)}), bf16[32,4,128]{2,1,0:T(4,128)(2,1)S(1)}, u32[]{:S(2)}, u32[]{:S(2)}) async-start(bf16[32,4,128]{2,1,0:T(4,128)(2,1)} %reshape.196), calls=%async_computation.3 | async-start | bytes 65536 | tf_op jit(solution)/shard_map/all_to_all | solution.py:103
  135.8 5.8 %collective-permute-start.2 = (bf16[32,96,128]{2,1,0:T(8,128)(2,1)S(1)}, bf16[32,96,128]{2,1,0:T(8,128)(2,1)S(1)}, u32[]{:S(2)}, u32[]{:S(2)}) collective-permute-start(bf16[32,96,128]{2,1,0:T(8,128)(2,1)S(1)} %all_to_all.25.mine_ref), channel_id=1, source_target_pairs={{0,1},{1,0},{2,3},{3,2},{4,5},{5,4},{6,7},{7,6},{8,9},{9,8},{10,11... | collective-permute-start | bytes 2359304 | tf_op jit(solution)/shard_map/ppermute | solution.py:242
  138.6 3.0 %copy-start = (bf16[288,12288]{1,0:T(8,128)(2,1)S(1)}, bf16[288,12288]{1,0:T(8,128)(2,1)}, u32[]{:S(2)}) copy-start(bf16[288,12288]{1,0:T(8,128)(2,1)} %get-tuple-element.8.weights_ref) | copy-start | bytes 21233668

commit v7 on v6

--- a/solution.py
+++ b/solution.py
@@ -34,10 +34,10 @@
 FAR = [
     [
         (2 * pair + plane) * 64 + place(2 * a + e, 2 * b + w, core)
-        for plane in range(2)
         for a in range(2)
         for b in range(4)
         for core in range(2)
+        for plane in range(2)
     ]
     for pair in range(8)
     for e in range(2)
@@ -204,10 +204,12 @@
     core = lax.rem(lax.axis_index("gy"), 2)
     plane = lax.rem(lax.axis_index("gx"), 2)
     width = tokens.shape[1]
-    split = tokens.reshape(4, 2, 2, width).transpose(1, 2, 0, 3)
-    far = jnp.broadcast_to(split[:, None], (2, 8, 2, 4, width)).reshape(CHIPS, 4, width)
-    far = exchange(far, ("gx", "gy"), FAR).reshape(2, 64, width)
-    rows = jnp.concatenate([far[0], far[1]], axis=1)
+    split = tokens.reshape(4, 2, 2, width).transpose(2, 1, 0, 3)
+    far = jnp.broadcast_to(split[None], (8, 2, 2, 4, width)).reshape(CHIPS, 4, width)
+    far = exchange(far, ("gx", "gy"), FAR).reshape(16, 2, 4, width)
+    rows = jnp.concatenate(
+        [far[:, 0].reshape(64, width), far[:, 1].reshape(64, width)], axis=1
+    )
     gathered = exchange(jnp.broadcast_to(rows[None], (4,) + rows.shape), "gy", NEAR)
     next_weight = lax.ppermute(qkv_weight, "gx", NEXT_PLANE)
     own_columns = jnp.concatenate(

time: 145 us -> 145 us (level)
  no operation moved by 1% of the time
where the time goes in v7:
time: 145 us; the launch traced here: 144 us
  starting transfers between devices  47.5 us (33%)
  waiting for transfers between devices  43.6 us (30%)
  blocking collectives  28.6 us (20%)
  Pallas kernels  12.4 us (9%)
  local copies, waits for them, and re-layouts  6.97 us (5%)
  matrix products  2.61 us (2%)
  between operations  1.55 us (1%)
    all_to_all x3, waiting for transfers between devices, exchange(): lax.all_to_all(blocks, axis, split_axis=0, concat_axis=0, axis_index_grou...  37.1 us
    all_to_all x3, starting transfers between devices, exchange(): lax.all_to_all(blocks, axis, split_axis=0, concat_axis=0, axis_index_grou...  31.6 us
    all_to_all x1, blocking collectives, exchange(): lax.all_to_all(blocks, axis, split_axis=0, concat_axis=0, axis_index_grou...  28.6 us
    pallas_call x1, Pallas kernels, copy_weights(): pl.pallas_call(copy_kernel, out_shape=(jax.ShapeDtypeStruct(core.shape, c...  9.53 us
    all_to_all x1, starting transfers between devices, on_device(): lax.all_to_all(partial_value.reshape(2, 16, 8, columns), 'gx', split_axis...  7.85 us
    all_to_all x1, waiting for transfers between devices, on_device(): lax.all_to_all(partial_value.reshape(2, 16, 8, columns), 'gx', split_axis...  4.32 us
    ppermute x1, starting transfers between devices, on_device(): theirs = lax.ppermute(mine, 'gy', SIBLING)  3.14 us
    unnamed x7, local copies, waits for them, and re-layouts  3.02 us
  transfers between devices with their start and end apart: 7, of which 5 were waited for; matrix products, arithmetic and copies ran while one was open for 1% of the time, Pallas kernels for 7%

profile of v7, /device:TPU:19, one launch (start us, length us, event | category | flops | bytes accessed | tf_op | source)
XLA Modules:
  0.0 143.9 jit_solution(16434406033722881782)
XLA Ops:
  0.0 0.8 reshape.190
  0.8 0.8 broadcast_in_dim.17
  1.6 21.7 %all-to-all-start = ((bf16[32,4,1152]{2,1,0:T(4,128)(2,1)}), bf16[32,4,1152]{2,1,0:T(4,128)(2,1)S(1)}, u32[]{:S(2)}, u32[]{:S(2)}) async-start(bf16[32,4,1152]{2,1,0:T(4,128)(2,1)} %bitcast.5), calls=%async_computation | async-start | bytes 589824 | tf_op jit(solution)/shard_map/all_to_all | solution.py:103
  23.3 2.0 %collective-permute-start = (bf16[1152,200]{0,1:T(8,128)(2,1)}, bf16[1152,200]{0,1:T(8,128)(2,1)S(1)}, u32[]{:S(2)}, u32[]{:S(2)}) collective-permute-start(bf16[1152,200]{0,1:T(8,128)(2,1)} %param.6), channel_id=1, source_target_pairs={{0,64},{64,0},{128,192},{192,128},{256,320},{320,256},{384,448},{4... | collective-permute-start | bytes 1382408 | tf_op jit(solution)/shard_map/ppermute | solution.py:214
  25.3 14.9 %all-to-all-done = bf16[32,4,1152]{2,1,0:T(4,128)(2,1)S(1)} async-done(((bf16[32,4,1152]{2,1,0:T(4,128)(2,1)}), bf16[32,4,1152]{2,1,0:T(4,128)(2,1)S(1)}, u32[]{:S(2)}, u32[]{:S(2)}) %all-to-all-start) | async-done | bytes 294944 | tf_op jit(solution)/shard_map/all_to_all | solution.py:103
  40.3 0.1 fusion.28
  40.5 1.1 broadcast_in_dim.18
  41.6 3.5 %all-to-all-start.1 = ((bf16[4,64,2304]{2,1,0:T(8,128)(2,1)}), bf16[4,64,2304]{2,1,0:T(8,128)(2,1)S(1)}, u32[]{:S(2)}, u32[]{:S(2)}) async-start(bf16[4,64,2304]{2,1,0:T(8,128)(2,1)} %broadcast_in_dim.18), calls=%async_computation.1 | async-start | bytes 2359296 | tf_op jit(solution)/shard_map/all_to_all | solution.py:103
  45.2 0.1 broadcast_select_fusion.1
  45.4 2.9 %collective-permute-start.1 = (bf16[2304,200]{0,1:T(8,128)(2,1)S(1)}, bf16[2304,200]{0,1:T(8,128)(2,1)S(1)}, u32[]{:S(2)}, u32[]{:S(2)}) collective-permute-start(bf16[2304,200]{0,1:T(8,128)(2,1)S(1)} %pad_maximum_fusion), channel_id=1, source_target_pairs={{0,1},{1,0},{2,3},{3,2},{4,5},{5,4},{6,7},{7,6},{8,9},{9,8},{10,11... | collective-permute-start | bytes 2764808 | tf_op jit(solution)/shard_map/ppermute | solution.py:222
  48.3 2.1 %collective-permute-done.1 = bf16[2304,200]{0,1:T(8,128)(2,1)S(1)} collective-permute-done((bf16[2304,200]{0,1:T(8,128)(2,1)S(1)}, bf16[2304,200]{0,1:T(8,128)(2,1)S(1)}, u32[]{:S(2)}, u32[]{:S(2)}) %collective-permute-start.1) | collective-permute-done | bytes 921632 | tf_op jit(solution)/shard_map/ppermute | solution.py:222
  50.4 11.2 %all-to-all-done.1 = bf16[4,64,2304]{2,1,0:T(8,128)(2,1)S(1)} async-done(((bf16[4,64,2304]{2,1,0:T(8,128)(2,1)}), bf16[4,64,2304]{2,1,0:T(8,128)(2,1)S(1)}, u32[]{:S(2)}, u32[]{:S(2)}) %all-to-all-start.1) | async-done | bytes 1179680 | tf_op jit(solution)/shard_map/all_to_all | solution.py:103
  61.5 1.6 %fusion.1 = f32[2,16,8,400]{3,2,0,1:T(8,128)} fusion(bf16[2304,200]{0,1:T(8,128)(2,1)S(1)} %collective-permute-done.1, bf16[1152,200]{0,1:T(8,128)(2,1)S(1)} %get-tuple-element.10, bf16[1152,200]{0,1:T(8,128)(2,1)S(1)} %get-tuple-element.9, bf16[2,16,8,2304]{3,2,1,0:T(8,128)(2,1)S(1)} %bitcast.45), kind=kOutput, calls=%fused_computation.3 | convolution fusion | flops 477388800 | bytes 3432448 | tf_op jit(solution)/shard_map/dot_general | solution.py:223
  63.1 7.8 %all-to-all-start.2 = ((f32[2,16,8,400]{3,2,0,1:T(8,128)}), f32[2,16,8,400]{3,2,0,1:T(8,128)S(1)}, u32[]{:S(2)}, u32[]{:S(2)}) async-start(f32[2,16,8,400]{3,2,0,1:T(8,128)} %fusion.1), calls=%async_computation.2 | async-start | bytes 1048576 | tf_op jit(solution)/shard_map/all_to_all | solution.py:227
  71.7 9.5 %shard_map.55 = (s32[1]{0:T(128)}, bf16[288,12288]{1,0:T(8,128)(2,1)}) custom-call(s32[1]{0:T(128)} %bitcast.core_ref, bf16[288,12288]{1,0:T(8,128)(2,1)} %bitcast.43), custom_call_target="tpu_custom_call" | custom-call | bytes 14155776 | tf_op jit(solution)/shard_map/pallas_call | solution.py:151
  81.8 4.3 %all-to-all-done.2 = f32[2,16,8,400]{3,2,0,1:T(8,128)S(1)} async-done(((f32[2,16,8,400]{3,2,0,1:T(8,128)}), f32[2,16,8,400]{3,2,0,1:T(8,128)S(1)}, u32[]{:S(2)}, u32[]{:S(2)}) %all-to-all-start.2) | async-done | bytes 409632 | tf_op jit(solution)/shard_map/all_to_all | solution.py:227
  86.3 0.1 fusion.29
  86.4 0.1 fusion.16
  86.5 0.6 reshape.195
  87.1 6.4 %all-to-all-start.3 = ((bf16[32,4,128]{2,1,0:T(4,128)(2,1)}), bf16[32,4,128]{2,1,0:T(4,128)(2,1)S(1)}, u32[]{:S(2)}, u32[]{:S(2)}) async-start(bf16[32,4,128]{2,1,0:T(4,128)(2,1)} %reshape.195), calls=%async_computation.3 | async-start | bytes 65536 | tf_op jit(solution)/shard_map/all_to_all | solution.py:103
  93.5 11.0 %all-to-all-done.3 = bf16[32,4,128]{2,1,0:T(4,128)(2,1)S(1)} async-done(((bf16[32,4,128]{2,1,0:T(4,128)(2,1)}), bf16[32,4,128]{2,1,0:T(4,128)(2,1)S(1)}, u32[]{:S(2)}, u32[]{:S(2)}) %all-to-all-start.3) | async-done | bytes 32800 | tf_op jit(solution)/shard_map/all_to_all | solution.py:103
  104.6 0.1 reshape.197
  104.7 0.1 fusion.17
  105.0 0.5 fusion.30
  105.5 0.1 fusion.31
  105.6 0.2 fusion.13
  105.9 0.4 fusion.7
  106.3 0.1 broadcast_in_dim.25
  106.4 28.6 %all_to_all.25.mine_ref = bf16[32,96,128]{2,1,0:T(8,128)(2,1)S(1)} all-to-all(bf16[32,96,128]{2,1,0:T(8,128)(2,1)S(1)} %broadcast_in_dim.25), channel_id=1, replica_groups={{0,2,4,6,8,10,12,14,16,18,20,22,24,26,28,30,32,34,36,38,40,42,44,46,48,..., dimensions={0} | all-to-all | bytes 1572864 | tf_op jit(solution)/shard_map/all_to_all | solution.py:103
  135.0 3.1 %collective-permute-start.2 = (bf16[32,96,128]{2,1,0:T(8,128)(2,1)S(1)}, bf16[32,96,128]{2,1,0:T(8,128)(2,1)S(1)}, u32[]{:S(2)}, u32[]{:S(2)}) collective-permute-start(bf16[32,96,128]{2,1,0:T(8,128)(2,1)S(1)} %all_to_all.25.mine_ref), channel_id=1, source_target_pairs={{0,1},{1,0},{2,3},{3,2},{4,5},{5,4},{6,7},{7,6},{8,9},{9,8},{10,11... | collective-permute-start | bytes 2359304 | tf_op jit(solution)/shard_map/ppermute | solution.py:244
  138.1 3.0 %copy-done = bf16[288,12288]{1,0:T(8,128)(2,1)S(1)} copy-done((bf16[288,12288]{1,0:T(8,128)(2,1)S(1)}, bf16[288,12288]{1,0:T(8,128)(2,1)}, u32[]{:S(2)}) %copy-start) | copy-done | bytes 7077912
  141.1 2.8 %shard_map.57 = bf16[64,288]{1,0:T(8,128)(2,1)} custom-call(s32[1]{0:T(128)} %bitcast.core_ref, bf16[32,96,128]{2,1,0:T(8,128)(2,1)S(1)} %all_to_all.25.mine_ref, bf16[32,96,128]{2,1,0:T(8,128)(2,1)S(1)} %collective-permute-done.2.theirs_ref, bf16[288,12288]{1,0:T(8,128)(2,1)S(1)} %shard_map.56.weights_ref), custom_call_target="tpu_custom_call" | custom-call | flops 452984832 | bytes 7077888 | tf_op jit(solution)/shard_map/pallas_call | solution.py:189
  (28 shorter events, 0.5 us)
Async XLA Ops:
  1.6 38.7 %all-to-all-start = ((bf16[32,4,1152]{2,1,0:T(4,128)(2,1)}), bf16[32,4,1152]{2,1,0:T(4,128)(2,1)S(1)}, u32[]{:S(2)}, u32[]{:S(2)}) async-start(bf16[32,4,1152]{2,1,0:T(4,128)(2,1)} %bitcast.5), calls=%async_computation | async-start | bytes 589824 | tf_op jit(solution)/shard_map/all_to_all | solution.py:103
  23.3 21.8 %collective-permute-start = (bf16[1152,200]{0,1:T(8,128)(2,1)}, bf16[1152,200]{0,1:T(8,128)(2,1)S(1)}, u32[]{:S(2)}, u32[]{:S(2)}) collective-permute-start(bf16[1152,200]{0,1:T(8,128)(2,1)} %param.6), channel_id=1, source_target_pairs={{0,64},{64,0},{128,192},{192,128},{256,320},{320,256},{384,448},{4... | collective-permute-start | bytes 1382408 | tf_op jit(solution)/shard_map/ppermute | solution.py:214
  40.5 4.7 %copy-start.1 = (bf16[1152,200]{0,1:T(8,128)(2,1)S(1)}, bf16[1152,200]{0,1:T(8,128)(2,1)}, u32[]{:S(2)}) copy-start(bf16[1152,200]{0,1:T(8,128)(2,1)} %param.6) | copy-start | bytes 1382404
  41.6 19.9 %all-to-all-start.1 = ((bf16[4,64,2304]{2,1,0:T(8,128)(2,1)}), bf16[4,64,2304]{2,1,0:T(8,128)(2,1)S(1)}, u32[]{:S(2)}, u32[]{:S(2)}) async-start(bf16[4,64,2304]{2,1,0:T(8,128)(2,1)} %broadcast_in_dim.18), calls=%async_computation.1 | async-start | bytes 2359296 | tf_op jit(solution)/shard_map/all_to_all | solution.py:103
  45.4 5.0 %collective-permute-start.1 = (bf16[2304,200]{0,1:T(8,128)(2,1)S(1)}, bf16[2304,200]{0,1:T(8,128)(2,1)S(1)}, u32[]{:S(2)}, u32[]{:S(2)}) collective-permute-start(bf16[2304,200]{0,1:T(8,128)(2,1)S(1)} %pad_maximum_fusion), channel_id=1, source_target_pairs={{0,1},{1,0},{2,3},{3,2},{4,5},{5,4},{6,7},{7,6},{8,9},{9,8},{10,11... | collective-permute-start | bytes 2764808 | tf_op jit(solution)/shard_map/ppermute | solution.py:222
  63.1 23.0 %all-to-all-start.2 = ((f32[2,16,8,400]{3,2,0,1:T(8,128)}), f32[2,16,8,400]{3,2,0,1:T(8,128)S(1)}, u32[]{:S(2)}, u32[]{:S(2)}) async-start(f32[2,16,8,400]{3,2,0,1:T(8,128)} %fusion.1), calls=%async_computation.2 | async-start | bytes 1048576 | tf_op jit(solution)/shard_map/all_to_all | solution.py:227
  71.6 33.3 %copy-start.2 = (bf16[1,2,2048,256]{3,2,1,0:T(8,128)(2,1)S(1)}, bf16[1,2,2048,256]{3,2,1,0:T(8,128)(2,1)}, u32[]{:S(2)}) copy-start(bf16[1,2,2048,256]{3,2,1,0:T(8,128)(2,1)} %param.8) | copy-start | bytes 6291460
  87.1 17.5 %all-to-all-start.3 = ((bf16[32,4,128]{2,1,0:T(4,128)(2,1)}), bf16[32,4,128]{2,1,0:T(4,128)(2,1)S(1)}, u32[]{:S(2)}, u32[]{:S(2)}) async-start(bf16[32,4,128]{2,1,0:T(4,128)(2,1)} %reshape.195), calls=%async_computation.3 | async-start | bytes 65536 | tf_op jit(solution)/shard_map/all_to_all | solution.py:103
  135.0 6.2 %collective-permute-start.2 = (bf16[32,96,128]{2,1,0:T(8,128)(2,1)S(1)}, bf16[32,96,128]{2,1,0:T(8,128)(2,1)S(1)}, u32[]{:S(2)}, u32[]{:S(2)}) collective-permute-start(bf16[32,96,128]{2,1,0:T(8,128)(2,1)S(1)} %all_to_all.25.mine_ref), channel_id=1, source_target_pairs={{0,1},{1,0},{2,3},{3,2},{4,5},{5,4},{6,7},{7,6},{8,9},{9,8},{10,11... | collective-permute-start | bytes 2359304 | tf_op jit(solution)/shard_map/ppermute | solution.py:244
  138.1 3.0 %copy-start = (bf16[288,12288]{1,0:T(8,128)(2,1)S(1)}, bf16[288,12288]{1,0:T(8,128)(2,1)}, u32[]{:S(2)}) copy-start(bf16[288,12288]{1,0:T(8,128)(2,1)} %get-tuple-element.8.weights_ref) | copy-start | bytes 21233668

commit v8 on v7

--- a/solution.py
+++ b/solution.py
@@ -108,10 +108,10 @@
 CHUNKS = 6
 
 
-def output_kernel(core_ref, mine_ref, theirs_ref, weights_ref, out_ref):
+def output_kernel(core_ref, mine_ref, theirs_ref, lower_ref, upper_ref, out_ref):
     tiles = mine_ref.shape[1] // CHUNKS
     depth = tiles * mine_ref.shape[2]
-    total = jnp.zeros((weights_ref.shape[0], 2 * CHIPS), jnp.float32)
+    total = jnp.zeros((lower_ref.shape[0], 2 * CHIPS), jnp.float32)
     for i in range(CHUNKS):
         here = slice(i * tiles, (i + 1) * tiles)
         rows = jnp.concatenate(
@@ -121,8 +121,9 @@
             ],
             axis=0,
         )
+        half, k = (lower_ref, i) if i < CHUNKS // 2 else (upper_ref, i - CHUNKS // 2)
         total += lax.dot_general(
-            weights_ref[:, i * depth : (i + 1) * depth],
+            half[:, k * depth : (k + 1) * depth],
             rows,
             (((1,), (1,)), ((), ())),
             preferred_element_type=jnp.float32,
@@ -140,23 +141,28 @@
     ).astype(jnp.bfloat16)
 
 
-def copy_kernel(core_ref, weights_ref, same_core_ref, copied_ref):
+def copy_kernel(core_ref, weights_ref, same_core_ref, lower_ref, upper_ref):
+    half = lower_ref.shape[1]
     same_core_ref[0] = core_ref[0]
-    copied_ref[...] = weights_ref[...]
+    lower_ref[...] = weights_ref[:, :half]
+    upper_ref[...] = weights_ref[:, half:]
 
 
 def copy_weights(core, weights):
     smem = pl.BlockSpec(memory_space=pltpu.SMEM)
     rows = pl.BlockSpec((32, weights.shape[1]), lambda step: (step, 0))
+    half_rows = pl.BlockSpec((32, weights.shape[1] // 2), lambda step: (step, 0))
+    half = jax.ShapeDtypeStruct((weights.shape[0], weights.shape[1] // 2), weights.dtype)
     return pl.pallas_call(
         copy_kernel,
         out_shape=(
             jax.ShapeDtypeStruct(core.shape, core.dtype),
-            jax.ShapeDtypeStruct(weights.shape, weights.dtype),
+            half,
+            half,
         ),
         grid=(weights.shape[0] // 32,),
         in_specs=[smem, rows],
-        out_specs=(smem, rows),
+        out_specs=(smem, half_rows, half_rows),
         compiler_params=pltpu.CompilerParams(vmem_limit_bytes=54 * 2**20),
         cost_estimate=pl.CostEstimate(
             flops=0, bytes_accessed=4 * weights.size, transcendentals=0
@@ -183,13 +189,13 @@
     )(weights)
 
 
-def output_rows(core, mine, theirs, weights):
-    columns, depth = weights.shape
+def output_rows(core, mine, theirs, lower, upper):
+    columns, depth = lower.shape[0], 2 * lower.shape[1]
     vmem = pl.BlockSpec(memory_space=pltpu.VMEM)
     return pl.pallas_call(
         output_kernel,
         out_shape=jax.ShapeDtypeStruct((2 * CHIPS, columns), jnp.bfloat16),
-        in_specs=[pl.BlockSpec(memory_space=pltpu.SMEM), vmem, vmem, vmem],
+        in_specs=[pl.BlockSpec(memory_space=pltpu.SMEM), vmem, vmem, vmem, vmem],
         out_specs=vmem,
         compiler_params=pltpu.CompilerParams(vmem_limit_bytes=32 * 2**20),
         cost_estimate=pl.CostEstimate(
@@ -197,7 +203,7 @@
             bytes_accessed=2 * columns * depth,
             transcendentals=0,
         ),
-    )(core.astype(jnp.int32).reshape(1), mine, theirs, weights)
+    )(core.astype(jnp.int32).reshape(1), mine, theirs, lower, upper)
 
 
 def on_device(tokens, qkv_weight, out_weight, cache, cache_lengths):
@@ -234,7 +240,7 @@
     )
     summed = jnp.sum(parts.reshape(2, 8, 2, 8, columns), axis=1)
     summed = summed.transpose(0, 2, 1, 3).reshape(CHIPS, columns)
-    same_core, turned = copy_weights(core.astype(jnp.int32).reshape(1), out_weight.T)
+    same_core, lower, upper = copy_weights(core.astype(jnp.int32).reshape(1), out_weight.T)
     summed = jnp.where(same_core[0] == 0, summed, jnp.roll(summed, columns // 2, axis=1))
     summed = jnp.pad(summed.astype(jnp.bfloat16), ((0, 0), (0, 512 - columns)))
     proj = exchange(summed.reshape(CHIPS, 4, 128), "gy", PLANE).reshape(CHIPS, 512)
@@ -242,7 +248,7 @@
     attended_output = attend_cached_keys(proj, cache, cache_lengths).reshape(1, 96, 128)
     mine = exchange(jnp.broadcast_to(attended_output, (CHIPS, 96, 128)), "gy", PLANE)
     theirs = lax.ppermute(mine, "gy", SIBLING)
-    return output_rows(core, mine, theirs, hold(turned))
+    return output_rows(core, mine, theirs, lower, hold(upper))
 
 
 def solution(mesh):

time: 145 us -> 148 us (1.021)
  matrix products: 2.61 us -> 4.58 us
  waiting for transfers between devices: 43.6 us -> 45.4 us
    unnamed x7 -> x9, local copies, waits for them, and re-layouts: 3.02 us -> 0.15 us
    broadcast_in_dim x2, local copies, waits for them, and re-layouts: 0.12 us -> 2.21 us  [on_device(): jnp.broadcast_to(attended_output, (CHIPS, 96, 128))]
    dot_general x1, matrix products: 0.36 us -> 2.33 us  [attend_cached_keys(): jnp.einsum('trj,tjp->trp', softmax_weights, cache[:, 1], preferred_elemen...]
    ppermute x1, waiting for transfers between devices: 0.01 us -> 1.86 us  [on_device(): theirs = lax.ppermute(mine, 'gy', SIBLING)]
  transfers between devices with their start and end apart: 7 -> 7, of which waited for: 5 -> 6; matrix products, arithmetic and copies ran while one was open for 1% -> 1% of each run, Pallas kernels for 7% -> 6%
where the time goes in v8:
time: 148 us; the launch traced here: 147 us
  starting transfers between devices  47.5 us (32%)
  waiting for transfers between devices  45.4 us (31%)
  blocking collectives  28.6 us (19%)
  Pallas kernels  12.4 us (8%)
  local copies, waits for them, and re-layouts  6.2 us (4%)
  matrix products  4.58 us (3%)
  between operations  1.55 us (1%)
    all_to_all x3, waiting for transfers between devices, exchange(): lax.all_to_all(blocks, axis, split_axis=0, concat_axis=0, axis_index_grou...  37.1 us
    all_to_all x3, starting transfers between devices, exchange(): lax.all_to_all(blocks, axis, split_axis=0, concat_axis=0, axis_index_grou...  31.6 us
    all_to_all x1, blocking collectives, exchange(): lax.all_to_all(blocks, axis, split_axis=0, concat_axis=0, axis_index_grou...  28.6 us
    pallas_call x1, Pallas kernels, copy_weights(): pl.pallas_call(copy_kernel, out_shape=(jax.ShapeDtypeStruct(core.shape, c...  9.54 us
    all_to_all x1, starting transfers between devices, on_device(): lax.all_to_all(partial_value.reshape(2, 16, 8, columns), 'gx', split_axis...  7.85 us
    all_to_all x1, waiting for transfers between devices, on_device(): lax.all_to_all(partial_value.reshape(2, 16, 8, columns), 'gx', split_axis...  4.32 us
    ppermute x1, starting transfers between devices, on_device(): theirs = lax.ppermute(mine, 'gy', SIBLING)  3.14 us
  transfers between devices with their start and end apart: 7, of which 6 were waited for; matrix products, arithmetic and copies ran while one was open for 1% of the time, Pallas kernels for 6%

profile of v8, /device:TPU:19, one launch (start us, length us, event | category | flops | bytes accessed | tf_op | source)
XLA Modules:
  0.0 147.0 jit_solution(5027489025028319617)
XLA Ops:
  0.0 0.8 reshape.190
  0.8 0.8 broadcast_in_dim.17
  1.6 21.7 %all-to-all-start = ((bf16[32,4,1152]{2,1,0:T(4,128)(2,1)}), bf16[32,4,1152]{2,1,0:T(4,128)(2,1)S(1)}, u32[]{:S(2)}, u32[]{:S(2)}) async-start(bf16[32,4,1152]{2,1,0:T(4,128)(2,1)} %bitcast.5), calls=%async_computation | async-start | bytes 589824 | tf_op jit(solution)/shard_map/all_to_all | solution.py:103
  23.3 2.0 %collective-permute-start = (bf16[1152,200]{0,1:T(8,128)(2,1)}, bf16[1152,200]{0,1:T(8,128)(2,1)S(1)}, u32[]{:S(2)}, u32[]{:S(2)}) collective-permute-start(bf16[1152,200]{0,1:T(8,128)(2,1)} %param.6), channel_id=1, source_target_pairs={{0,64},{64,0},{128,192},{192,128},{256,320},{320,256},{384,448},{4... | collective-permute-start | bytes 1382408 | tf_op jit(solution)/shard_map/ppermute | solution.py:220
  25.3 14.9 %all-to-all-done = bf16[32,4,1152]{2,1,0:T(4,128)(2,1)S(1)} async-done(((bf16[32,4,1152]{2,1,0:T(4,128)(2,1)}), bf16[32,4,1152]{2,1,0:T(4,128)(2,1)S(1)}, u32[]{:S(2)}, u32[]{:S(2)}) %all-to-all-start) | async-done | bytes 294944 | tf_op jit(solution)/shard_map/all_to_all | solution.py:103
  40.3 0.1 fusion.28
  40.5 1.1 broadcast_in_dim.18
  41.6 3.5 %all-to-all-start.1 = ((bf16[4,64,2304]{2,1,0:T(8,128)(2,1)}), bf16[4,64,2304]{2,1,0:T(8,128)(2,1)S(1)}, u32[]{:S(2)}, u32[]{:S(2)}) async-start(bf16[4,64,2304]{2,1,0:T(8,128)(2,1)} %broadcast_in_dim.18), calls=%async_computation.1 | async-start | bytes 2359296 | tf_op jit(solution)/shard_map/all_to_all | solution.py:103
  45.2 0.1 broadcast_select_fusion.1
  45.4 2.9 %collective-permute-start.1 = (bf16[2304,200]{0,1:T(8,128)(2,1)S(1)}, bf16[2304,200]{0,1:T(8,128)(2,1)S(1)}, u32[]{:S(2)}, u32[]{:S(2)}) collective-permute-start(bf16[2304,200]{0,1:T(8,128)(2,1)S(1)} %pad_maximum_fusion), channel_id=1, source_target_pairs={{0,1},{1,0},{2,3},{3,2},{4,5},{5,4},{6,7},{7,6},{8,9},{9,8},{10,11... | collective-permute-start | bytes 2764808 | tf_op jit(solution)/shard_map/ppermute | solution.py:228
  48.3 2.1 %collective-permute-done.1 = bf16[2304,200]{0,1:T(8,128)(2,1)S(1)} collective-permute-done((bf16[2304,200]{0,1:T(8,128)(2,1)S(1)}, bf16[2304,200]{0,1:T(8,128)(2,1)S(1)}, u32[]{:S(2)}, u32[]{:S(2)}) %collective-permute-start.1) | collective-permute-done | bytes 921632 | tf_op jit(solution)/shard_map/ppermute | solution.py:228
  50.4 11.2 %all-to-all-done.1 = bf16[4,64,2304]{2,1,0:T(8,128)(2,1)S(1)} async-done(((bf16[4,64,2304]{2,1,0:T(8,128)(2,1)}), bf16[4,64,2304]{2,1,0:T(8,128)(2,1)S(1)}, u32[]{:S(2)}, u32[]{:S(2)}) %all-to-all-start.1) | async-done | bytes 1179680 | tf_op jit(solution)/shard_map/all_to_all | solution.py:103
  61.5 1.6 %fusion.1 = f32[2,16,8,400]{3,2,0,1:T(8,128)} fusion(bf16[2304,200]{0,1:T(8,128)(2,1)S(1)} %collective-permute-done.1, bf16[1152,200]{0,1:T(8,128)(2,1)S(1)} %get-tuple-element.12, bf16[1152,200]{0,1:T(8,128)(2,1)S(1)} %get-tuple-element.11, bf16[2,16,8,2304]{3,2,1,0:T(8,128)(2,1)S(1)} %bitcast.45), kind=kOutput, calls=%fused_computation.3 | convolution fusion | flops 477388800 | bytes 3432448 | tf_op jit(solution)/shard_map/dot_general | solution.py:229
  63.1 7.8 %all-to-all-start.2 = ((f32[2,16,8,400]{3,2,0,1:T(8,128)}), f32[2,16,8,400]{3,2,0,1:T(8,128)S(1)}, u32[]{:S(2)}, u32[]{:S(2)}) async-start(f32[2,16,8,400]{3,2,0,1:T(8,128)} %fusion.1), calls=%async_computation.2 | async-start | bytes 1048576 | tf_op jit(solution)/shard_map/all_to_all | solution.py:233
  71.7 9.5 %shard_map.55 = (s32[1]{0:T(128)}, bf16[288,6144]{1,0:T(8,128)(2,1)}, bf16[288,6144]{1,0:T(8,128)(2,1)}) custom-call(s32[1]{0:T(128)} %bitcast.core_ref, bf16[288,12288]{1,0:T(8,128)(2,1)} %bitcast.43), custom_call_target="tpu_custom_call" | custom-call | bytes 14155776 | tf_op jit(solution)/shard_map/pallas_call | solution.py:156
  81.9 4.3 %all-to-all-done.2 = f32[2,16,8,400]{3,2,0,1:T(8,128)S(1)} async-done(((f32[2,16,8,400]{3,2,0,1:T(8,128)}), f32[2,16,8,400]{3,2,0,1:T(8,128)S(1)}, u32[]{:S(2)}, u32[]{:S(2)}) %all-to-all-start.2) | async-done | bytes 409632 | tf_op jit(solution)/shard_map/all_to_all | solution.py:233
  86.5 0.6 reshape.195
  87.1 6.4 %all-to-all-start.3 = ((bf16[32,4,128]{2,1,0:T(4,128)(2,1)}), bf16[32,4,128]{2,1,0:T(4,128)(2,1)S(1)}, u32[]{:S(2)}, u32[]{:S(2)}) async-start(bf16[32,4,128]{2,1,0:T(4,128)(2,1)} %reshape.195), calls=%async_computation.3 | async-start | bytes 65536 | tf_op jit(solution)/shard_map/all_to_all | solution.py:103
  93.5 11.0 %all-to-all-done.3 = bf16[32,4,128]{2,1,0:T(4,128)(2,1)S(1)} async-done(((bf16[32,4,128]{2,1,0:T(4,128)(2,1)}), bf16[32,4,128]{2,1,0:T(4,128)(2,1)S(1)}, u32[]{:S(2)}, u32[]{:S(2)}) %all-to-all-start.3) | async-done | bytes 32800 | tf_op jit(solution)/shard_map/all_to_all | solution.py:103
  104.6 0.1 reshape.197
  104.7 0.1 fusion.17
  105.0 0.5 fusion.30
  105.5 0.1 fusion.31
  105.6 0.2 fusion.13
  105.9 2.3 %fusion.7 = bf16[48,256]{1,0:T(8,128)(2,1)} fusion(bf16[1,2,2048,256]{3,2,1,0:T(8,128)(2,1)} %param.8, f32[48,2048]{1,0:T(8,128)S(1)} %get-tuple-element.26, f32[48]{0:T(128)S(1)} %get-tuple-element.22, f32[48]{0:T(128)S(1)} %get-tuple-element.27, f32[256]{0:T(256)S(1)} %bitcast.51, f32[48]{0:T(128)S(1)} %get-tuple-element.21), kind=kOutput, calls=%fused_computation.10 | convolution fusion | flops 50663424 | bytes 1467968 | tf_op jit(solution)/shard_map/trj,tjp->trp/dot_general | solution.py:92
  108.2 1.4 broadcast_in_dim.24
  109.6 0.8 broadcast_in_dim.25
  110.5 28.6 %all_to_all.25.mine_ref = bf16[32,96,128]{2,1,0:T(8,128)(2,1)S(1)} all-to-all(bf16[32,96,128]{2,1,0:T(8,128)(2,1)S(1)} %broadcast_in_dim.25), channel_id=1, replica_groups={{0,2,4,6,8,10,12,14,16,18,20,22,24,26,28,30,32,34,36,38,40,42,44,46,48,..., dimensions={0} | all-to-all | bytes 1572864 | tf_op jit(solution)/shard_map/all_to_all | solution.py:103
  139.0 3.1 %collective-permute-start.2 = (bf16[32,96,128]{2,1,0:T(8,128)(2,1)S(1)}, bf16[32,96,128]{2,1,0:T(8,128)(2,1)S(1)}, u32[]{:S(2)}, u32[]{:S(2)}) collective-permute-start(bf16[32,96,128]{2,1,0:T(8,128)(2,1)S(1)} %all_to_all.25.mine_ref), channel_id=1, source_target_pairs={{0,1},{1,0},{2,3},{3,2},{4,5},{5,4},{6,7},{7,6},{8,9},{9,8},{10,11... | collective-permute-start | bytes 2359304 | tf_op jit(solution)/shard_map/ppermute | solution.py:250
  142.2 1.9 %collective-permute-done.2.theirs_ref = bf16[32,96,128]{2,1,0:T(8,128)(2,1)S(1)} collective-permute-done((bf16[32,96,128]{2,1,0:T(8,128)(2,1)S(1)}, bf16[32,96,128]{2,1,0:T(8,128)(2,1)S(1)}, u32[]{:S(2)}, u32[]{:S(2)}) %collective-permute-start.2) | collective-permute-done | bytes 786464 | tf_op jit(solution)/shard_map/ppermute | solution.py:250
  144.1 0.1 copy-done.1
  144.2 2.8 %shard_map.57 = bf16[64,288]{1,0:T(8,128)(2,1)} custom-call(s32[1]{0:T(128)} %bitcast.core_ref, bf16[32,96,128]{2,1,0:T(8,128)(2,1)S(1)} %all_to_all.25.mine_ref, bf16[32,96,128]{2,1,0:T(8,128)(2,1)S(1)} %collective-permute-done.2.theirs_ref, bf16[288,6144]{1,0:T(8,128)(2,1)S(1)} %copy-done.1, bf16[288,6144]{1,0:T(8,128)(2,1)S(1)} %shard_map.56.upper_ref), custom_call_target="tpu_custom_call" | custom-call | flops 452984832 | bytes 7077888 | tf_op jit(solution)/shard_map/pallas_call | solution.py:195
  (30 shorter events, 0.7 us)
Async XLA Ops:
  1.6 38.7 %all-to-all-start = ((bf16[32,4,1152]{2,1,0:T(4,128)(2,1)}), bf16[32,4,1152]{2,1,0:T(4,128)(2,1)S(1)}, u32[]{:S(2)}, u32[]{:S(2)}) async-start(bf16[32,4,1152]{2,1,0:T(4,128)(2,1)} %bitcast.5), calls=%async_computation | async-start | bytes 589824 | tf_op jit(solution)/shard_map/all_to_all | solution.py:103
  23.3 21.8 %collective-permute-start = (bf16[1152,200]{0,1:T(8,128)(2,1)}, bf16[1152,200]{0,1:T(8,128)(2,1)S(1)}, u32[]{:S(2)}, u32[]{:S(2)}) collective-permute-start(bf16[1152,200]{0,1:T(8,128)(2,1)} %param.6), channel_id=1, source_target_pairs={{0,64},{64,0},{128,192},{192,128},{256,320},{320,256},{384,448},{4... | collective-permute-start | bytes 1382408 | tf_op jit(solution)/shard_map/ppermute | solution.py:220
  40.5 4.7 %copy-start.2 = (bf16[1152,200]{0,1:T(8,128)(2,1)S(1)}, bf16[1152,200]{0,1:T(8,128)(2,1)}, u32[]{:S(2)}) copy-start(bf16[1152,200]{0,1:T(8,128)(2,1)} %param.6) | copy-start | bytes 1382404
  41.6 19.9 %all-to-all-start.1 = ((bf16[4,64,2304]{2,1,0:T(8,128)(2,1)}), bf16[4,64,2304]{2,1,0:T(8,128)(2,1)S(1)}, u32[]{:S(2)}, u32[]{:S(2)}) async-start(bf16[4,64,2304]{2,1,0:T(8,128)(2,1)} %broadcast_in_dim.18), calls=%async_computation.1 | async-start | bytes 2359296 | tf_op jit(solution)/shard_map/all_to_all | solution.py:103
  45.4 5.0 %collective-permute-start.1 = (bf16[2304,200]{0,1:T(8,128)(2,1)S(1)}, bf16[2304,200]{0,1:T(8,128)(2,1)S(1)}, u32[]{:S(2)}, u32[]{:S(2)}) collective-permute-start(bf16[2304,200]{0,1:T(8,128)(2,1)S(1)} %pad_maximum_fusion), channel_id=1, source_target_pairs={{0,1},{1,0},{2,3},{3,2},{4,5},{5,4},{6,7},{7,6},{8,9},{9,8},{10,11... | collective-permute-start | bytes 2764808 | tf_op jit(solution)/shard_map/ppermute | solution.py:228
  63.1 23.0 %all-to-all-start.2 = ((f32[2,16,8,400]{3,2,0,1:T(8,128)}), f32[2,16,8,400]{3,2,0,1:T(8,128)S(1)}, u32[]{:S(2)}, u32[]{:S(2)}) async-start(f32[2,16,8,400]{3,2,0,1:T(8,128)} %fusion.1), calls=%async_computation.2 | async-start | bytes 1048576 | tf_op jit(solution)/shard_map/all_to_all | solution.py:233
  71.6 33.3 %copy-start.3 = (bf16[1,2,2048,256]{3,2,1,0:T(8,128)(2,1)S(1)}, bf16[1,2,2048,256]{3,2,1,0:T(8,128)(2,1)}, u32[]{:S(2)}) copy-start(bf16[1,2,2048,256]{3,2,1,0:T(8,128)(2,1)} %param.8) | copy-start | bytes 6291460
  87.1 17.4 %all-to-all-start.3 = ((bf16[32,4,128]{2,1,0:T(4,128)(2,1)}), bf16[32,4,128]{2,1,0:T(4,128)(2,1)S(1)}, u32[]{:S(2)}, u32[]{:S(2)}) async-start(bf16[32,4,128]{2,1,0:T(4,128)(2,1)} %reshape.195), calls=%async_computation.3 | async-start | bytes 65536 | tf_op jit(solution)/shard_map/all_to_all | solution.py:103
  105.9 36.3 %copy-start = (bf16[288,6144]{1,0:T(8,128)(2,1)S(1)}, bf16[288,6144]{1,0:T(8,128)(2,1)}, u32[]{:S(2)}) copy-start(bf16[288,6144]{1,0:T(8,128)(2,1)} %get-tuple-element.10.weights_ref) | copy-start | bytes 10616836
  139.0 5.0 %collective-permute-start.2 = (bf16[32,96,128]{2,1,0:T(8,128)(2,1)S(1)}, bf16[32,96,128]{2,1,0:T(8,128)(2,1)S(1)}, u32[]{:S(2)}, u32[]{:S(2)}) collective-permute-start(bf16[32,96,128]{2,1,0:T(8,128)(2,1)S(1)} %all_to_all.25.mine_ref), channel_id=1, source_target_pairs={{0,1},{1,0},{2,3},{3,2},{4,5},{5,4},{6,7},{7,6},{8,9},{9,8},{10,11... | collective-permute-start | bytes 2359304 | tf_op jit(solution)/shard_map/ppermute | solution.py:250
  142.2 2.0 %copy-start.1 = (bf16[288,6144]{1,0:T(8,128)(2,1)S(1)}, bf16[288,6144]{1,0:T(8,128)(2,1)}, u32[]{:S(2)}) copy-start(bf16[288,6144]{1,0:T(8,128)(2,1)} %get-tuple-element.9.lower_ref) | copy-start | bytes 10616836
